TPU v7x, 256 devices: a whole 4x4x8 slice. The times are simulated.
256 devices in a mesh: slot: 64 (over y_lo, z, x), head: 4 (over y_hi, core).
Axes of the slice: x: 4, y: 4 (y_hi: 2, y_lo: 2; y = y_hi * 2 + y_lo), z: 8, core: 2. Of those that a mesh axis runs over, the one named last changes fastest.
Arguments:
- queries: bfloat16 [4096, 6144], P('slot', 'head'), may hold values from -4.5 to 4.5
- keys: bfloat16 [4096, 1024], P('slot', 'head'), may hold values from -4.5 to 4.5
- values: bfloat16 [4096, 1024], P('slot', 'head'), may hold values from -4.5 to 4.5
- cache_keys: bfloat16 [16384, 1024], P('slot', 'head'), may hold values from -4.5 to 4.5
- cache_values: bfloat16 [16384, 1024], P('slot', 'head'), may hold values from -4.5 to 4.5
- cache_count: int32 [64], P('slot'), may hold values from 1 to 240
- span_section: int32 [4], replicated, may hold values from 0 to 3, each once
- norm_gain: float32 [6144], P('head'), may hold values from 0.5 to 1.5
Outputs:
- attended: float32 [4096, 6144], P('slot', 'head')
- new_cache_keys: bfloat16 [16384, 1024], P('slot', 'head')
- new_cache_values: bfloat16 [16384, 1024], P('slot', 'head')
Inputs may be any that keep to these rules, and one draw needn't show every extreme that they name: `span_section`: the noise section of each group; 0 marks the span that retires.
All inputs are finite; a program needn't handle non-finite values.
Results may differ from a plain program's by a relative error of at most 0.0085.
Values may be sent and summed in bfloat16 or wider, within the bound.
A program may use at most 64 MiB of HBM per device.

v0:
```python
import jax
import jax.numpy as jnp
from jax import lax
from jax.sharding import PartitionSpec as P

HEADS = 48
HEAD = 128


def for_sending(shard):
    return jax.tree.map(lambda a: a.astype(jnp.bfloat16) if a.dtype == jnp.float32 else a, shard)


def from_partner(block, axis, stride):
    count = lax.axis_size(axis)
    route = []
    for low in range(count):
        high = low | 1 << stride
        if high != low and high < count:
            route += [(low, high), (high, low)]
    return lax.ppermute(block, axis, route)


def bit_high(index, bit):
    return index // (1 << bit) % 2 == 1


def partial_attention(query_rows, key_rows, value_rows, visible):
    rows = query_rows.shape[0]
    heads_here = query_rows.shape[1] // HEAD
    sharing = query_rows.shape[1] // key_rows.shape[1]

    def head_step(head_idx, carry):
        numer, top, total = carry
        start = head_idx * HEAD
        kv_start = head_idx // sharing * HEAD
        query_h = lax.dynamic_slice_in_dim(query_rows, start, HEAD, 1)
        key_h = lax.dynamic_slice_in_dim(key_rows, kv_start, HEAD, 1)
        value_h = lax.dynamic_slice_in_dim(value_rows, kv_start, HEAD, 1)
        score = jnp.einsum(
            "qd,kd->qk", query_h, key_h, preferred_element_type=jnp.float32
        ) * HEAD ** (-0.5)
        score = jnp.where(visible[None, :], score, -1e30)
        peak = jnp.max(score, axis=1)
        expo = jnp.where(visible[None, :], jnp.exp(score - peak[:, None]), 0.0)
        mixed = jnp.dot(expo.astype(jnp.bfloat16), value_h, preferred_element_type=jnp.float32)
        numer = lax.dynamic_update_slice_in_dim(numer, mixed, start, 1)
        top = lax.dynamic_update_slice_in_dim(top, peak[:, None], head_idx, 1)
        total = lax.dynamic_update_slice_in_dim(total, jnp.sum(expo, axis=1)[:, None], head_idx, 1)
        return (numer, top, total)

    start_carry = (
        jnp.zeros((rows, heads_here * HEAD), jnp.float32),
        jnp.zeros((rows, heads_here), jnp.float32),
        jnp.zeros((rows, heads_here), jnp.float32),
    )
    return lax.fori_loop(0, heads_here, head_step, start_carry)


def combine(first, second):
    numer_a, top_a, total_a = first
    numer_b, top_b, total_b = second
    rows = numer_a.shape[0]
    top = jnp.maximum(top_a, top_b)
    factor_a = jnp.exp(top_a - top)
    factor_b = jnp.exp(top_b - top)
    numer = (
        numer_a.reshape(rows, -1, HEAD) * factor_a[:, :, None]
        + numer_b.reshape(rows, -1, HEAD) * factor_b[:, :, None]
    ).reshape(rows, -1)
    return (numer, top, total_a * factor_a + total_b * factor_b)


def on_device(
    queries, keys, values, cache_keys, cache_values, cache_count, span_section, norm_gain
):
    slots = lax.axis_size("slot")
    group_size = slots // 4
    group_bits = group_size.bit_length() - 1
    index = lax.axis_index("slot")
    my_group = index // group_size
    tok_rows = queries.shape[0]
    cache_rows = cache_keys.shape[0]
    quarter = tok_rows // 4
    count = cache_count[0]
    cache_flag = (jnp.arange(cache_rows) < count).astype(jnp.bfloat16)
    my_section = span_section[my_group]
    own_parts = (keys, values, cache_keys, cache_values, cache_flag)
    parts = own_parts
    for bit in range(group_bits, group_bits + 2):
        other = jax.tree.map(
            lambda part, own: part.astype(own.dtype),
            from_partner(for_sending(parts), "slot", bit),
            parts,
        )
        high = bit_high(index, bit)
        parts = tuple(
            (
                jnp.where(high, jnp.concatenate([theirs, mine]), jnp.concatenate([mine, theirs]))
                for mine, theirs in zip(parts, other)
            )
        )
    source = jnp.arange(4, dtype=jnp.int32)
    column_keys, column_values, column_cache_keys, column_cache_values, column_flags = parts
    retiring = jnp.sum(
        jnp.arange(4, dtype=jnp.int32) * (span_section[source] == 0).astype(jnp.int32)
    )
    retire_start = retiring * tok_rows + my_group * quarter
    retired_keys = lax.dynamic_slice_in_dim(column_keys, retire_start, quarter, 0)
    retired_values = lax.dynamic_slice_in_dim(column_values, retire_start, quarter, 0)
    zero_index = jnp.zeros((), jnp.int32)
    new_cache_keys = lax.dynamic_update_slice(cache_keys, retired_keys, (count, zero_index))
    new_cache_values = lax.dynamic_update_slice(cache_values, retired_values, (count, zero_index))
    span_seen = jnp.repeat((span_section[source] <= my_section).astype(jnp.bfloat16), tok_rows)
    key_rows = jnp.concatenate([column_keys, column_cache_keys])
    value_rows = jnp.concatenate([column_values, column_cache_values])
    seen_flags = jnp.concatenate([span_seen, column_flags])
    gathered = queries
    for bit in range(group_bits):
        other = from_partner(gathered, "slot", bit)
        high = bit_high(index, bit)
        gathered = jnp.where(
            high, jnp.concatenate([other, gathered]), jnp.concatenate([gathered, other])
        )
    state = partial_attention(gathered, key_rows, value_rows, seen_flags > 0.5)
    for bit in reversed(range(group_bits)):
        half = state[0].shape[0] // 2
        high = bit_high(index, bit)
        keep = tuple((jnp.where(high, item[half:], item[:half]) for item in state))
        send = tuple((jnp.where(high, item[:half], item[half:]) for item in state))
        other = from_partner((send[0], send[1], send[2]), "slot", bit)
        state = combine(keep, other)
    numer, top, total = state
    mixed = (numer.reshape(tok_rows, -1, HEAD) / total[:, :, None]).reshape(tok_rows, -1)
    squares = lax.psum(jnp.sum(mixed * mixed, axis=1), "head")
    meansq = squares / (HEADS * HEAD)
    attended = mixed * lax.rsqrt(meansq + 1e-06)[:, None] * norm_gain[None, :]
    return (attended, new_cache_keys, new_cache_values)


def solution(mesh):
    placed = (
        P("slot", "head"),
        P("slot", "head"),
        P("slot", "head"),
        P("slot", "head"),
        P("slot", "head"),
        P("slot"),
        P(),
        P("head"),
    )
    return jax.shard_map(
        on_device,
        mesh=mesh,
        in_specs=placed,
        out_specs=(P("slot", "head"), P("slot", "head"), P("slot", "head")),
        check_vma=False,
    )
```

profile of v0, /device:TPU:1, one launch (start us, length us, event | category | flops | bytes accessed | tf_op | source)
XLA Modules:
  0.0 478.4 jit_solution(1956065840571067695)
XLA Ops:
  4.6 3.6 collective-permute-done.2
  9.3 4.0 collective-permute-start.3
  13.3 6.9 %collective-permute-done.3 = bf16[128,1536]{1,0:T(8,128)(2,1)S(1)} collective-permute-done((bf16[128,1536]{1,0:T(8,128)(2,1)S(1)}, bf16[128,1536]{1,0:T(8,128)(2,1)S(1)}, u32[]{:S(2)}, u32[]{:S(2)}) %collective-permute-start.3) | collective-permute-done | bytes 393248 | tf_op jit(solution)/shard_map/ppermute | solution.py:21
  20.3 2.7 collective-permute-start.4
  23.6 6.1 %collective-permute-start = (bf16[256]{0:T(256)(128)(2,1)S(1)}, bf16[256]{0:T(256)(128)(2,1)S(1)}, u32[]{:S(2)}, u32[]{:S(2)}) collective-permute-start(bf16[256]{0:T(256)(128)(2,1)S(1)} %compare_convert_fusion), channel_id=1, source_target_pairs={{0,64},{64,0},{4,68},{68,4},{8,72},{72,8},{12,76},{76,12},{16,80},... | collective-permute-start | bytes 1544 | tf_op jit(solution)/shard_map/ppermute | solution.py:21
  29.8 5.3 %collective-permute-start.10 = (bf16[64,256]{1,0:T(8,128)(2,1)}, bf16[64,256]{1,0:T(8,128)(2,1)S(1)}, u32[]{:S(2)}, u32[]{:S(2)}) collective-permute-start(bf16[64,256]{1,0:T(8,128)(2,1)} %param.12), channel_id=1, source_target_pairs={{0,64},{64,0},{4,68},{68,4},{8,72},{72,8},{12,76},{76,12},{16,80},... | collective-permute-start | bytes 98312 | tf_op jit(solution)/shard_map/ppermute | solution.py:21
  37.9 5.8 %collective-permute-done = bf16[256]{0:T(256)(128)(2,1)S(1)} collective-permute-done((bf16[256]{0:T(256)(128)(2,1)S(1)}, bf16[256]{0:T(256)(128)(2,1)S(1)}, u32[]{:S(2)}, u32[]{:S(2)}) %collective-permute-start) | collective-permute-done | bytes 544 | tf_op jit(solution)/shard_map/ppermute | solution.py:21
  46.3 3.2 collective-permute-start.5
  51.3 2.6 collective-permute-done.8
  56.0 3.6 collective-permute-done.9
  59.8 2.3 collective-permute-done.13
  62.5 62.7 %collective-permute-done.5 = bf16[512,1536]{1,0:T(8,128)(2,1)S(1)} collective-permute-done((bf16[512,1536]{1,0:T(8,128)(2,1)S(1)}, bf16[512,1536]{1,0:T(8,128)(2,1)S(1)}, u32[]{:S(2)}, u32[]{:S(2)}) %collective-permute-start.5) | collective-permute-done | bytes 1572896 | tf_op jit(solution)/shard_map/ppermute | solution.py:21
  125.2 2.3 maximum_select_fusion
  127.4 3.4 broadcast_in_dim.87.clone
  130.9 119.2 %while.19 = (s32[]{:T(128)}, f32[1024,1536]{0,1:T(8,128)}, f32[1024,12]{0,1:T(8,128)S(1)}, f32[1024,12]{0,1:T(8,128)S(1)}, pred[1280]{0:T(1024)(128)(4,1)S(1)}, ...) while((s32[]{:T(128)}, f32[1024,1536]{0,1:T(8,128)}, ...), condition=%wide.region_3.4_spmd, body=%wide.region_0.3_spmd.sunk | while | flops 682883072 | bytes 38180468 | solution.py:57
  132.8 2.3 copy-done.1
  136.4 4.4 fusion.36
  142.8 2.3 copy-done.1
  146.4 4.4 fusion.36
  152.7 2.3 copy-done.1
  156.3 4.4 fusion.36
  162.7 2.3 copy-done.1
  166.3 4.3 fusion.36
  172.6 2.3 copy-done.1
  176.2 4.4 fusion.36
  182.5 2.3 copy-done.1
  186.1 4.3 fusion.36
  192.4 2.3 copy-done.1
  196.0 4.4 fusion.36
  202.4 2.3 copy-done.1
  206.0 4.4 fusion.36
  212.3 2.3 copy-done.1
  215.9 4.4 fusion.36
  222.3 2.3 copy-done.1
  225.9 4.4 fusion.36
  232.2 2.3 copy-done.1
  235.8 4.3 fusion.36
  242.1 2.3 copy-done.1
  245.7 4.4 fusion.36
  250.1 3.6 slice_select_fusion.1
  253.8 2.4 collective-permute-start.14
  256.3 136.6 %collective-permute-done.14 = f32[512,12]{0,1:T(8,128)S(1)} collective-permute-done((f32[512,12]{0,1:T(8,128)S(1)}, f32[512,12]{0,1:T(8,128)S(1)}, u32[]{:S(2)}, u32[]{:S(2)}) %collective-permute-start.14) | collective-permute-done | bytes 24608 | tf_op jit(solution)/shard_map/ppermute | solution.py:21
  400.0 32.1 %collective-permute-done.16 = f32[256,12]{0,1:T(8,128)S(1)} collective-permute-done((f32[256,12]{0,1:T(8,128)}, f32[256,12]{0,1:T(8,128)S(1)}, u32[]{:S(2)}, u32[]{:S(2)}) %collective-permute-start.16) | collective-permute-done | bytes 12320 | tf_op jit(solution)/shard_map/ppermute | solution.py:21
  433.3 2.9 collective-permute-start.18
  438.3 2.8 collective-permute-start.24
  441.1 16.1 %collective-permute-done.24 = f32[128,12]{0,1:T(8,128)S(1)} collective-permute-done((f32[128,12]{0,1:T(8,128)S(1)}, f32[128,12]{0,1:T(8,128)S(1)}, u32[]{:S(2)}, u32[]{:S(2)}) %collective-permute-start.24) | collective-permute-done | bytes 6176 | tf_op jit(solution)/shard_map/ppermute | solution.py:21
  461.5 4.9 %collective-permute-done.20 = f32[64,12]{0,1:T(8,128)S(1)} collective-permute-done((f32[64,12]{0,1:T(8,128)S(1)}, f32[64,12]{0,1:T(8,128)S(1)}, u32[]{:S(2)}, u32[]{:S(2)}) %collective-permute-start.20) | collective-permute-done | bytes 3104 | tf_op jit(solution)/shard_map/ppermute | solution.py:21
  467.3 10.0 %psum.7 = f32[64]{0:T(128)S(1)} all-reduce(f32[64]{0:T(128)S(1)} %get-tuple-element.223), channel_id=1, replica_groups=mesh['slot'=64,'head'=4] {'head'}, use_global_device_ids=true, to_apply=%region_5.6 | all-reduce | flops 64 | bytes 512 | tf_op jit(solution)/shard_map/psum | solution.py:135
  (170 shorter events, 69.5 us)
Async XLA Ops:
  0.6 35.8 %copy-start = (s32[4]{0:T(128)S(1)}, s32[4]{0:T(128)}, u32[]{:S(2)}) copy-start(s32[4]{0:T(128)} %param.16) | copy-start | bytes 52
  1.6 53.8 %copy-start.3 = (bf16[256,256]{1,0:T(8,128)(2,1)}, bf16[256,256]{1,0:T(8,128)(2,1)S(1)}, u32[]{:S(2)}) copy-start(bf16[256,256]{1,0:T(8,128)(2,1)S(1)} %copy.52) | copy-start | bytes 393220
  2.5 5.6 %collective-permute-start.2 = (bf16[64,1536]{1,0:T(8,128)(2,1)}, bf16[64,1536]{1,0:T(8,128)(2,1)S(1)}, u32[]{:S(2)}, u32[]{:S(2)}) collective-permute-start(bf16[64,1536]{1,0:T(8,128)(2,1)} %param.10), channel_id=1, source_target_pairs={{0,4},{4,0},{8,12},{12,8},{16,20},{20,16},{24,28},{28,24},{32,36},... | collective-permute-start | bytes 589832 | tf_op jit(solution)/shard_map/ppermute | solution.py:21
  4.5 45.0 %copy-start.6 = (bf16[64,256]{1,0:T(8,128)(2,1)S(1)}, bf16[64,256]{1,0:T(8,128)(2,1)}, u32[]{:S(2)}) copy-start(bf16[64,256]{1,0:T(8,128)(2,1)} %param.12) | copy-start | bytes 98308
  4.5 46.5 %copy-start.7 = (bf16[64,256]{1,0:T(8,128)(2,1)S(1)}, bf16[64,256]{1,0:T(8,128)(2,1)}, u32[]{:S(2)}) copy-start(bf16[64,256]{1,0:T(8,128)(2,1)} %param.11) | copy-start | bytes 98308
  9.3 10.9 %collective-permute-start.3 = (bf16[128,1536]{1,0:T(8,128)(2,1)S(1)}, bf16[128,1536]{1,0:T(8,128)(2,1)S(1)}, u32[]{:S(2)}, u32[]{:S(2)}) collective-permute-start(bf16[128,1536]{1,0:T(8,128)(2,1)S(1)} %maximum_select_fusion.5), channel_id=1, source_target_pairs={{0,8},{8,0},{4,12},{12,4},{16,24},{24,16},{20,28},{28,20},{32,40},... | collective-permute-start | bytes 1179656 | tf_op jit(solution)/shard_map/ppermute | solution.py:21
  20.3 23.5 %collective-permute-start.4 = (bf16[256,1536]{1,0:T(8,128)(2,1)S(1)}, bf16[256,1536]{1,0:T(8,128)(2,1)S(1)}, u32[]{:S(2)}, u32[]{:S(2)}) collective-permute-start(bf16[256,1536]{1,0:T(8,128)(2,1)S(1)} %maximum_select_fusion.2), channel_id=1, source_target_pairs={{0,16},{16,0},{4,20},{20,4},{8,24},{24,8},{12,28},{28,12},{32,48},... | collective-permute-start | bytes 2359304 | tf_op jit(solution)/shard_map/ppermute | solution.py:21
  23.6 20.1 %collective-permute-start = (bf16[256]{0:T(256)(128)(2,1)S(1)}, bf16[256]{0:T(256)(128)(2,1)S(1)}, u32[]{:S(2)}, u32[]{:S(2)}) collective-permute-start(bf16[256]{0:T(256)(128)(2,1)S(1)} %compare_convert_fusion), channel_id=1, source_target_pairs={{0,64},{64,0},{4,68},{68,4},{8,72},{72,8},{12,76},{76,12},{16,80},... | collective-permute-start | bytes 1544 | tf_op jit(solution)/shard_map/ppermute | solution.py:21
  29.7 21.3 %collective-permute-start.6 = (bf16[64,256]{1,0:T(8,128)(2,1)}, bf16[64,256]{1,0:T(8,128)(2,1)S(1)}, u32[]{:S(2)}, u32[]{:S(2)}) collective-permute-start(bf16[64,256]{1,0:T(8,128)(2,1)} %param.11), channel_id=1, source_target_pairs={{0,64},{64,0},{4,68},{68,4},{8,72},{72,8},{12,76},{76,12},{16,80},... | collective-permute-start | bytes 98312 | tf_op jit(solution)/shard_map/ppermute | solution.py:21
  29.8 19.7 %collective-permute-start.10 = (bf16[64,256]{1,0:T(8,128)(2,1)}, bf16[64,256]{1,0:T(8,128)(2,1)S(1)}, u32[]{:S(2)}, u32[]{:S(2)}) collective-permute-start(bf16[64,256]{1,0:T(8,128)(2,1)} %param.12), channel_id=1, source_target_pairs={{0,64},{64,0},{4,68},{68,4},{8,72},{72,8},{12,76},{76,12},{16,80},... | collective-permute-start | bytes 98312 | tf_op jit(solution)/shard_map/ppermute | solution.py:21
  35.1 20.3 %collective-permute-start.12 = (bf16[256,256]{1,0:T(8,128)(2,1)S(1)}, bf16[256,256]{1,0:T(8,128)(2,1)S(1)}, u32[]{:S(2)}, u32[]{:S(2)}) collective-permute-start(bf16[256,256]{1,0:T(8,128)(2,1)S(1)} %copy.52), channel_id=1, source_target_pairs={{0,64},{64,0},{4,68},{68,4},{8,72},{72,8},{12,76},{76,12},{16,80},... | collective-permute-start | bytes 393224 | tf_op jit(solution)/shard_map/ppermute | solution.py:21
  37.1 25.2 %copy-start.9 = (s32[4]{0:T(128)}, s32[4]{0:T(128)S(1)}, u32[]{:S(2)}) copy-start(s32[4]{0:T(128)S(1)} %gather_fusion) | copy-start | bytes 52
  43.8 10.1 %collective-permute-start.8 = (bf16[256,256]{1,0:T(8,128)(2,1)S(1)}, bf16[256,256]{1,0:T(8,128)(2,1)S(1)}, u32[]{:S(2)}, u32[]{:S(2)}) collective-permute-start(bf16[256,256]{1,0:T(8,128)(2,1)S(1)} %copy.51), channel_id=1, source_target_pairs={{0,64},{64,0},{4,68},{68,4},{8,72},{72,8},{12,76},{76,12},{16,80},... | collective-permute-start | bytes 393224 | tf_op jit(solution)/shard_map/ppermute | solution.py:21
  43.8 2.5 collective-permute-start.1
  46.3 78.9 %collective-permute-start.5 = (bf16[512,1536]{1,0:T(8,128)(2,1)S(1)}, bf16[512,1536]{1,0:T(8,128)(2,1)S(1)}, u32[]{:S(2)}, u32[]{:S(2)}) collective-permute-start(bf16[512,1536]{1,0:T(8,128)(2,1)S(1)} %maximum_select_fusion.1), channel_id=1, source_target_pairs={{0,32},{32,0},{4,36},{36,4},{8,40},{40,8},{12,44},{44,12},{16,48},... | collective-permute-start | bytes 4718600 | tf_op jit(solution)/shard_map/ppermute | solution.py:21
  49.6 6.3 %collective-permute-start.11 = (bf16[128,256]{1,0:T(8,128)(2,1)S(1)}, bf16[128,256]{1,0:T(8,128)(2,1)S(1)}, u32[]{:S(2)}, u32[]{:S(2)}) collective-permute-start(bf16[128,256]{1,0:T(8,128)(2,1)S(1)} %maximum_select_fusion.11), channel_id=1, source_target_pairs={{0,128},{128,0},{4,132},{132,4},{8,136},{136,8},{12,140},{140,12},... | collective-permute-start | bytes 196616 | tf_op jit(solution)/shard_map/ppermute | solution.py:21
  51.0 4.9 %collective-permute-start.7 = (bf16[128,256]{1,0:T(8,128)(2,1)S(1)}, bf16[128,256]{1,0:T(8,128)(2,1)S(1)}, u32[]{:S(2)}, u32[]{:S(2)}) collective-permute-start(bf16[128,256]{1,0:T(8,128)(2,1)S(1)} %maximum_select_fusion.10), channel_id=1, source_target_pairs={{0,128},{128,0},{4,132},{132,4},{8,136},{136,8},{12,140},{140,12},... | collective-permute-start | bytes 196616 | tf_op jit(solution)/shard_map/ppermute | solution.py:21
  54.0 5.6 %collective-permute-start.9 = (bf16[512,256]{1,0:T(8,128)(2,1)S(1)}, bf16[512,256]{1,0:T(8,128)(2,1)S(1)}, u32[]{:S(2)}, u32[]{:S(2)}) collective-permute-start(bf16[512,256]{1,0:T(8,128)(2,1)S(1)} %maximum_select_fusion.6), channel_id=1, source_target_pairs={{0,128},{128,0},{4,132},{132,4},{8,136},{136,8},{12,140},{140,12},... | collective-permute-start | bytes 786440 | tf_op jit(solution)/shard_map/ppermute | solution.py:21
  55.5 6.6 %collective-permute-start.13 = (bf16[512,256]{1,0:T(8,128)(2,1)S(1)}, bf16[512,256]{1,0:T(8,128)(2,1)S(1)}, u32[]{:S(2)}, u32[]{:S(2)}) collective-permute-start(bf16[512,256]{1,0:T(8,128)(2,1)S(1)} %maximum_select_fusion.7), channel_id=1, source_target_pairs={{0,128},{128,0},{4,132},{132,4},{8,136},{136,8},{12,140},{140,12},... | collective-permute-start | bytes 786440 | tf_op jit(solution)/shard_map/ppermute | solution.py:21
  132.8 2.3 copy-start.1
  142.8 2.3 copy-start.1
  152.7 2.3 copy-start.1
  162.7 2.3 copy-start.1
  172.6 2.3 copy-start.1
  182.5 2.3 copy-start.1
  192.4 2.3 copy-start.1
  202.4 2.3 copy-start.1
  212.3 2.3 copy-start.1
  222.3 2.3 copy-start.1
  232.2 2.3 copy-start.1
  242.1 2.3 copy-start.1
  253.7 140.0 %collective-permute-start.15 = (f32[512,1536]{0,1:T(8,128)S(1)}, f32[512,1536]{0,1:T(8,128)S(1)}, u32[]{:S(2)}, u32[]{:S(2)}) collective-permute-start(f32[512,1536]{0,1:T(8,128)S(1)} %get-tuple-element.243), channel_id=1, source_target_pairs={{0,32},{32,0},{4,36},{36,4},{8,40},{40,8},{12,44},{44,12},{16,48},... | collective-permute-start | bytes 9437192 | tf_op jit(solution)/shard_map/ppermute | solution.py:21
  253.8 139.1 %collective-permute-start.14 = (f32[512,12]{0,1:T(8,128)S(1)}, f32[512,12]{0,1:T(8,128)S(1)}, u32[]{:S(2)}, u32[]{:S(2)}) collective-permute-start(f32[512,12]{0,1:T(8,128)S(1)} %slice_select_fusion.6), channel_id=1, source_target_pairs={{0,32},{32,0},{4,36},{36,4},{8,40},{40,8},{12,44},{44,12},{16,48},... | collective-permute-start | bytes 73736 | tf_op jit(solution)/shard_map/ppermute | solution.py:21
  256.2 137.4 %collective-permute-start.22 = (f32[512,12]{0,1:T(8,128)S(1)}, f32[512,12]{0,1:T(8,128)S(1)}, u32[]{:S(2)}, u32[]{:S(2)}) collective-permute-start(f32[512,12]{0,1:T(8,128)S(1)} %slice_select_fusion.5), channel_id=1, source_target_pairs={{0,32},{32,0},{4,36},{36,4},{8,40},{40,8},{12,44},{44,12},{16,48},... | collective-permute-start | bytes 73736 | tf_op jit(solution)/shard_map/ppermute | solution.py:21
  393.7 2.3 copy-start.5
  393.7 4.4 copy-start.4
  394.5 4.1 copy-start.10
  396.0 40.2 %collective-permute-start.17 = (f32[256,1536]{0,1:T(8,128)}, f32[256,1536]{0,1:T(8,128)}, u32[]{:S(2)}, u32[]{:S(2)}) collective-permute-start(f32[256,1536]{0,1:T(8,128)} %bitcast.6), channel_id=1, source_target_pairs={{0,16},{16,0},{4,20},{20,4},{8,24},{24,8},{12,28},{28,12},{32,48},... | collective-permute-start | bytes 4718600 | tf_op jit(solution)/shard_map/ppermute | solution.py:21
  396.6 35.5 %collective-permute-start.16 = (f32[256,12]{0,1:T(8,128)}, f32[256,12]{0,1:T(8,128)S(1)}, u32[]{:S(2)}, u32[]{:S(2)}) collective-permute-start(f32[256,12]{0,1:T(8,128)} %slice_select_fusion.9), channel_id=1, source_target_pairs={{0,16},{16,0},{4,20},{20,4},{8,24},{24,8},{12,28},{28,12},{32,48},... | collective-permute-start | bytes 36872 | tf_op jit(solution)/shard_map/ppermute | solution.py:21
  398.6 33.8 %collective-permute-start.23 = (f32[256,12]{0,1:T(8,128)}, f32[256,12]{0,1:T(8,128)}, u32[]{:S(2)}, u32[]{:S(2)}) collective-permute-start(f32[256,12]{0,1:T(8,128)} %slice_select_fusion.8), channel_id=1, source_target_pairs={{0,16},{16,0},{4,20},{20,4},{8,24},{24,8},{12,28},{28,12},{32,48},... | collective-permute-start | bytes 36872 | tf_op jit(solution)/shard_map/ppermute | solution.py:21
  433.3 7.8 %collective-permute-start.18 = (f32[128,12]{0,1:T(8,128)S(1)}, f32[128,12]{0,1:T(8,128)S(1)}, u32[]{:S(2)}, u32[]{:S(2)}) collective-permute-start(f32[128,12]{0,1:T(8,128)S(1)} %slice_select_fusion.15), channel_id=1, source_target_pairs={{0,8},{8,0},{4,12},{12,4},{16,24},{24,16},{20,28},{28,20},{32,40},... | collective-permute-start | bytes 18440 | tf_op jit(solution)/shard_map/ppermute | solution.py:21
  438.0 19.3 %collective-permute-start.19 = (f32[128,1536]{0,1:T(8,128)S(1)}, f32[128,1536]{0,1:T(8,128)S(1)}, u32[]{:S(2)}, u32[]{:S(2)}) collective-permute-start(f32[128,1536]{0,1:T(8,128)S(1)} %bitcast.27), channel_id=1, source_target_pairs={{0,8},{8,0},{4,12},{12,4},{16,24},{24,16},{20,28},{28,20},{32,40},... | collective-permute-start | bytes 2359304 | tf_op jit(solution)/shard_map/ppermute | solution.py:21
  438.3 18.9 %collective-permute-start.24 = (f32[128,12]{0,1:T(8,128)S(1)}, f32[128,12]{0,1:T(8,128)S(1)}, u32[]{:S(2)}, u32[]{:S(2)}) collective-permute-start(f32[128,12]{0,1:T(8,128)S(1)} %slice_select_fusion.12), channel_id=1, source_target_pairs={{0,8},{8,0},{4,12},{12,4},{16,24},{24,16},{20,28},{28,20},{32,40},... | collective-permute-start | bytes 18440 | tf_op jit(solution)/shard_map/ppermute | solution.py:21
  457.8 19.8 %copy-start.8 = (f32[1536]{0:T(1024)S(1)}, f32[1536]{0:T(1024)}, u32[]{:S(2)}) copy-start(f32[1536]{0:T(1024)} %param.17) | copy-start | bytes 18436
  458.1 8.6 %collective-permute-start.21 = (f32[64,1536]{1,0:T(8,128)S(1)}, f32[64,1536]{1,0:T(8,128)S(1)}, u32[]{:S(2)}, u32[]{:S(2)}) collective-permute-start(f32[64,1536]{1,0:T(8,128)S(1)} %copy.25), channel_id=1, source_target_pairs={{0,4},{4,0},{8,12},{12,8},{16,20},{20,16},{24,28},{28,24},{32,36},... | collective-permute-start | bytes 1179656 | tf_op jit(solution)/shard_map/ppermute | solution.py:21
  458.5 7.9 %collective-permute-start.20 = (f32[64,12]{0,1:T(8,128)S(1)}, f32[64,12]{0,1:T(8,128)S(1)}, u32[]{:S(2)}, u32[]{:S(2)}) collective-permute-start(f32[64,12]{0,1:T(8,128)S(1)} %slice_select_fusion.13), channel_id=1, source_target_pairs={{0,4},{4,0},{8,12},{12,8},{16,20},{20,16},{24,28},{28,24},{32,36},... | collective-permute-start | bytes 9224 | tf_op jit(solution)/shard_map/ppermute | solution.py:21
  459.7 6.9 %collective-permute-start.25 = (f32[64,12]{0,1:T(8,128)S(1)}, f32[64,12]{0,1:T(8,128)S(1)}, u32[]{:S(2)}, u32[]{:S(2)}) collective-permute-start(f32[64,12]{0,1:T(8,128)S(1)} %slice_select_fusion.11), channel_id=1, source_target_pairs={{0,4},{4,0},{8,12},{12,8},{16,20},{20,16},{24,28},{28,24},{32,36},... | collective-permute-start | bytes 9224 | tf_op jit(solution)/shard_map/ppermute | solution.py:21
  461.5 17.0 %copy-start.2 = (bf16[256,256]{1,0:T(8,128)(2,1)}, bf16[256,256]{1,0:T(8,128)(2,1)S(1)}, u32[]{:S(2)}) copy-start(bf16[256,256]{1,0:T(8,128)(2,1)S(1)} %dynamic_update_slice.36) | copy-start | bytes 393220
where the time goes:
time: 480 us; the launch traced here: 478 us
  waiting for transfers between devices  279 us (58%)
  matrix products  76 us (16%)
  local copies, waits for them, and re-layouts  40.3 us (8%)
  starting transfers between devices  40.3 us (8%)
  other arithmetic  30.3 us (6%)
  blocking collectives  10 us (2%)
    ppermute x26, waiting for transfers between devices, from_partner(): return lax.ppermute(block, axis, route)  279 us
    dynamic_update_slice x12, matrix products, head_step(): numer = lax.dynamic_update_slice_in_dim(numer, mixed, start, 1)  52.4 us
    ppermute x26, starting transfers between devices, from_partner(): return lax.ppermute(block, axis, route)  40.3 us
    while x24, local copies, waits for them, and re-layouts  28 us
    dot_general x12, matrix products, head_step(): jnp.einsum('qd,kd->qk', query_h, key_h, preferred_element_type=jnp.float32)  23.7 us
    reduce_sum x12, other arithmetic, head_step(): jnp.sum(expo, axis=1)[:, None]  12.2 us
    psum x1, blocking collectives, on_device(): squares = lax.psum(jnp.sum(mixed * mixed, axis=1), 'head')  10 us
  transfers between devices with their start and end apart: 26, of which 15 were waited for; matrix products, arithmetic and copies ran while one was open for 2% of the time, Pallas kernels for 0%

commit v1 on v0

v1 whole, which is shorter than its diff:
```python
import functools

import jax
import jax.numpy as jnp
from jax import lax
from jax.experimental import pallas as pl
from jax.experimental.pallas import tpu as pltpu
from jax.sharding import PartitionSpec as P

MESH = pl.DeviceIdType.MESH
F32 = jnp.float32
BF16 = jnp.bfloat16

HEADS = 48
HEAD = 128
TOK = 64
CACHE = 256
KEYS = TOK + CACHE
KROWS = KEYS + 16
KCUT = 176
VCUT = 160
HERE = 12
SHARE = 6
W = HERE * HEAD
HALF = TOK // 2
LOG2E = 1.4426950408889634
C = HEAD ** -0.5 * LOG2E
NEG = -1e30
NZ, NX = 8, 4


def kernel(
    q_ref, k_ref, v_ref, ck_ref, cv_ref, gain_ref, count_ref, section_ref,
    out_ref, nck_ref, ncv_ref,
    qg, kbuf, vbuf, rbuf, bias, o_a, l_a, o_cur, l_cur, sbuf, mbuf, sq_s, sq_r,
    q_send, q_recv, k_send, k_recv, v_send, v_recv, r_send, r_recv, o_send, o_recv, s_send, s_recv,
):
    slot = lax.axis_index("slot")
    head = lax.axis_index("head")
    y = slot // 32
    z = slot // 4 % 8
    x = slot % 4

    def at(y_, z_, x_):
        return (y_ * 32 + z_ * 4 + x_, head)

    z_dev = (at(y, (z + 1) % NZ, x), at(y, (z + 7) % NZ, x))
    x_dev = (at(y, z, (x + 1) % NX), at(y, z, (x + 3) % NX))
    y_dev = at(1 - y, z, x)
    col_dev = (y_dev, at(y, (z + 4) % NZ, x), at(1 - y, (z + 4) % NZ, x))
    head_dev = tuple((slot, (head // 2 * 2 + (1 - head % 2), (head + 2) % 4, (head + 2) % 4 // 2 * 2 + (1 - head % 2))[i]) for i in range(3))

    barrier = pltpu.get_barrier_semaphore()
    peers = z_dev + x_dev + col_dev + head_dev
    for peer in peers:
        pl.semaphore_signal(barrier, inc=1, device_id=peer, device_id_type=MESH)

    qg[0] = q_ref[...]
    kbuf[0, 0, 0:TOK] = k_ref[...]
    kbuf[0, 0, TOK:KEYS] = ck_ref[...]
    kbuf[0, 0, KEYS:KROWS] = jnp.full((16, 256), count_ref[0].astype(F32), F32).astype(BF16)
    vbuf[0, 0, 0:TOK] = v_ref[...]
    vbuf[0, 0, TOK:KEYS] = cv_ref[...]
    pl.semaphore_wait(barrier, len(peers))

    def remote(src, dst, send, recv, dev):
        return pltpu.make_async_remote_copy(
            src_ref=src, dst_ref=dst, send_sem=send, recv_sem=recv, device_id=dev, device_id_type=MESH
        )

    def q_rows(ref, e, p):
        return ref.at[e, p * HALF:(p + 1) * HALF]

    def q_copy(d, step, p):
        src = (-step if d == 0 else step) % NZ
        dst = (-step - 1 if d == 0 else step + 1) % NZ
        return remote(q_rows(qg, src, p), q_rows(qg, dst, p), q_send.at[d, step, p], q_recv.at[d, step, p], z_dev[d])

    def k_copies():
        full = lambda h, s: kbuf.at[h, s]
        lo = lambda h, s: kbuf.at[h, s, 0:KCUT]
        hi = lambda h, s: kbuf.at[h, s, KCUT:KROWS]
        table = {
            "own_up": (full(0, 0), full(0, 1), x_dev[0]),
            "own_down": (full(0, 0), full(0, 2), x_dev[1]),
            "own_y": (full(0, 0), full(0, 3), y_dev),
            "fwd_up": (lo(0, 1), lo(1, 0), x_dev[0]),
            "fwd_down": (hi(0, 2), hi(1, 0), x_dev[1]),
            "y_up": (full(0, 3), full(1, 1), x_dev[0]),
            "y_down": (full(0, 3), full(1, 2), x_dev[1]),
            "yf_up": (lo(1, 1), lo(1, 3), x_dev[0]),
            "yf_down": (hi(1, 2), hi(1, 3), x_dev[1]),
        }
        return {n: remote(s, d, k_send.at[i], k_recv.at[i], dev) for i, (n, (s, d, dev)) in enumerate(table.items())}

    def v_copies():
        full = lambda h, s: vbuf.at[h, s]
        lo = lambda h, s: vbuf.at[h, s, 0:VCUT]
        hi = lambda h, s: vbuf.at[h, s, VCUT:KEYS]
        table = {
            "own_up": (full(0, 0), full(0, 1), x_dev[0]),
            "own_down": (full(0, 0), full(0, 2), x_dev[1]),
            "own_y": (full(0, 0), full(0, 3), y_dev),
            "fwd_up": (lo(0, 1), lo(1, 0), x_dev[0]),
            "fwd_down": (hi(0, 2), hi(1, 0), x_dev[1]),
            "y_1": (full(0, 1), full(1, 1), y_dev),
            "y_2": (full(0, 2), full(1, 2), y_dev),
            "y_3": (full(1, 0), full(1, 3), y_dev),
        }
        return {n: remote(s, d, v_send.at[i], v_recv.at[i], dev) for i, (n, (s, d, dev)) in enumerate(table.items())}

    kc, vc = k_copies(), v_copies()

    def retire_copies():
        out = []
        for i, dev in enumerate(col_dev):
            group = dev[0] // 16
            rows = pl.ds(pl.multiple_of(group * 16, 16), 16)
            out.append(remote(kbuf.at[0, 0, rows], rbuf.at[0, i], r_send.at[0, i], r_recv.at[0, i], dev))
            out.append(remote(vbuf.at[0, 0, rows], rbuf.at[1, i], r_send.at[1, i], r_recv.at[1, i], dev))
        return out

    rc = retire_copies()

    for p in (0, 1):
        for d in (0, 1):
            q_copy(d, 0, p if d == 0 else 1 - p).start()
            if p == 0:
                kc[("own_up", "own_down")[d]].start()
        if p == 0:
            kc["own_y"].start()
    vc["own_up"].start()
    vc["own_down"].start()
    vc["own_y"].start()
    for copy in rc:
        copy.start()

    def q_pass(step, first):
        for d in (0, 1):
            p = d if first else 1 - d
            q_copy(d, step, p).wait_recv()
            if step < 2 or (step == 2 and first):
                q_copy(d, step + 1, p).start()

    q_pass(0, True)
    q_pass(0, False)
    for n, f in (("own_up", "fwd_up"), ("own_down", "fwd_down")):
        kc[n].wait_recv()
        kc[f].start()
    kc["own_y"].wait_recv()
    kc["y_up"].start()
    kc["y_down"].start()
    q_pass(1, True)
    for n, f, t in (("own_up", "fwd_up", "y_1"), ("own_down", "fwd_down", "y_2")):
        vc[n].wait_recv()
        vc[f].start()
        vc[t].start()
    vc["own_y"].wait_recv()

    lane = lax.broadcasted_iota(jnp.int32, (1, 4 * KEYS), 1)

    def make_bias(half):
        for qhi in (0, 1):
            mine = section_ref[y * 2 + qhi]
            total = jnp.zeros((1, 4 * KEYS), F32)
            for s in range(4):
                other = (s == 3) if half == 0 else (s > 0)
                ky = 1 - y if other else y
                seen = section_ref[ky * 2 + z // 4] <= mine
                tok = jnp.where(seen, 0.0, NEG).astype(F32)
                live = kbuf[half, s, KEYS:KROWS, 0:128].astype(F32)[0:1, 0:1]
                row = lane - s * KEYS
                dead = jnp.where((row - TOK).astype(F32) >= live, NEG, 0.0)
                here = (row >= 0) & (row < KEYS)
                total = jnp.where(here, jnp.where(row < TOK, tok, dead), total)
            bias[half, qhi] = total

    ones = jnp.ones((4 * KEYS, HEAD), BF16)

    def attend(half, e, g):
        qhi = (z + e) % NZ // 4
        q = jnp.concatenate([qg[e, :, (g * SHARE + h) * HEAD:(g * SHARE + h + 1) * HEAD] for h in range(SHARE)], 0)
        k = jnp.concatenate([kbuf[half, s, 0:KEYS, g * HEAD:(g + 1) * HEAD] for s in range(4)], 0)
        v = jnp.concatenate([vbuf[half, s, :, g * HEAD:(g + 1) * HEAD] for s in range(4)], 0)
        score = lax.dot_general(q, k, (((1,), (1,)), ((), ())), preferred_element_type=F32)
        score = score + bias[half, qhi]
        top = jnp.max(score, axis=1, keepdims=True)
        weight = jnp.exp2((score - top) * C).astype(BF16)
        mixed = jnp.dot(weight, jnp.concatenate([v, ones], 1), preferred_element_type=F32)
        total = mixed[:, HEAD:]
        return mixed[:, :HEAD] / total, top * C + jnp.log2(total)

    def merge(o1, l1, o2, l2):
        top = jnp.maximum(l1, l2)
        w1 = jnp.exp2(l1 - top)
        w2 = jnp.exp2(l2 - top)
        total = w1 + w2
        return (o1 * w1 + o2 * w2) / total, top + jnp.log2(total)

    make_bias(0)

    def phase_a(i, carry):
        e = jnp.where(i % 2 == 1, NZ - (i + 1) // 2, i // 2)

        @pl.when(i == 1)
        def _():
            q_pass(1, False)

        @pl.when(i == 2)
        def _():
            q_pass(2, True)

        @pl.when(i == 3)
        def _():
            for n in ("fwd_up", "fwd_down"):
                kc[n].wait_recv()
                vc[n].wait_recv()
            vc["y_3"].start()

        @pl.when(i == 4)
        def _():
            for n, f in (("y_up", "yf_up"), ("y_down", "yf_down")):
                kc[n].wait_recv()
                kc[f].start()

        @pl.when(i == 5)
        def _():
            q_pass(2, False)

        @pl.when(i == 7)
        def _():
            q_pass(3, True)

        for g in (0, 1):
            o, l = attend(0, e, g)
            for h in range(SHARE):
                cols = slice((g * SHARE + h) * HEAD, (g * SHARE + h + 1) * HEAD)
                o_a[e, :, cols] = o[h * TOK:(h + 1) * TOK]
                l_a[e, :, cols] = l[h * TOK:(h + 1) * TOK]
        return carry

    lax.fori_loop(0, NZ, phase_a, 0)

    for n in ("yf_up", "yf_down"):
        kc[n].wait_recv()
    for n in ("y_1", "y_2", "y_3"):
        vc[n].wait_recv()
    make_bias(1)

    lane128 = lax.broadcasted_iota(jnp.int32, (HALF, HEAD), 1)

    def o_copy(d, step, p):
        rows = pl.ds(pl.multiple_of(p * HALF, HALF), HALF)
        dev = at(y, (z + 1 + 6 * d) % NZ, x)
        return remote(sbuf.at[d, step, rows], mbuf.at[d, step, rows], o_send.at[d, step, p], o_recv.at[d, step, p], dev)

    def read_message(d, step, p):
        o_copy(d, step, p).wait_recv()
        rows = pl.ds(pl.multiple_of(p * HALF, HALF), HALF)
        packed = mbuf[d, step, rows, W:W + HEAD].astype(F32)
        stat = packed + pltpu.roll(packed, HEAD - 16, 1) + pltpu.roll(packed, HEAD - 32, 1)
        return rows, stat

    def send_piece(d, step, p, combine):
        rows = pl.ds(pl.multiple_of(p * HALF, HALF), HALF)
        if combine:
            _, stat = read_message(d, step - 1, p)
        packed = jnp.zeros((HALF, HEAD), F32)
        for h in range(HERE):
            cols = slice(h * HEAD, (h + 1) * HEAD)
            o = o_cur[rows, cols]
            l = l_cur[rows, cols]
            if combine:
                o2 = mbuf[d, step - 1, rows, cols].astype(F32)
                l2 = jnp.broadcast_to(stat[:, h:h + 1], (HALF, HEAD))
                o, l = merge(o, l, o2, l2)
            sbuf[d, step, rows, cols] = o.astype(BF16)
            packed = jnp.where(lane128 % 16 == h, l, packed)
        first = packed.astype(BF16).astype(F32)
        rest = packed - first
        second = rest.astype(BF16).astype(F32)
        third = rest - second
        parts = jnp.where(lane128 < 16, first, jnp.where(lane128 < 32, second, third))
        parts = jnp.where(lane128 < 48, parts, 0.0)
        sbuf[d, step, rows, W:W + HEAD] = parts.astype(BF16)
        o_copy(d, step, p).start()

    def phase_b(i, carry):
        j = NZ - 1 - i
        e = jnp.where(j % 2 == 1, NZ - (j + 1) // 2, j // 2)
        for g in (0, 1):
            o, l = attend(1, e, g)
            for h in range(SHARE):
                cols = slice((g * SHARE + h) * HEAD, (g * SHARE + h + 1) * HEAD)
                part = slice(h * TOK, (h + 1) * TOK)
                o2, l2 = merge(o[part], l[part], o_a[e, :, cols], l_a[e, :, cols])
                o_cur[:, cols] = o2
                l_cur[:, cols] = l2

        d = 1 - i % 2
        step = (i + 1) // 2

        @pl.when(i == 0)
        def _():
            send_piece(0, 0, 0, False)
            send_piece(1, 0, 1, False)

        @pl.when((i > 0) & (i < 7))
        def _():
            send_piece(d, step, d, True)

        @pl.when((i > 0) & (i < 3))
        def _():
            send_piece(d, step, 1 - d, False)

        @pl.when((i > 2) & (i < 7))
        def _():
            send_piece(d, step, 1 - d, True)

        return carry

    lax.fori_loop(0, NZ, phase_b, 0)

    for p in (0, 1):
        rows = slice(p * HALF, (p + 1) * HALF)
        _, stat0 = read_message(0, 3, p)
        _, stat1 = read_message(1, 3, p)
        squares = jnp.zeros((HALF, HEAD), F32)
        for h in range(HERE):
            cols = slice(h * HEAD, (h + 1) * HEAD)
            o, l = o_cur[rows, cols], l_cur[rows, cols]
            for d, stat in ((0, stat0), (1, stat1)):
                l2 = jnp.broadcast_to(stat[:, h:h + 1], (HALF, HEAD))
                o, l = merge(o, l, mbuf[d, 3, rows, cols].astype(F32), l2)
            o_cur[rows, cols] = o
            squares = squares + o * o
        sq_s[rows, :] = jnp.broadcast_to(jnp.sum(squares, axis=1, keepdims=True), (HALF, HEAD))
    sc = [remote(sq_s, sq_r.at[i], s_send.at[i], s_recv.at[i], head_dev[i]) for i in range(3)]
    for copy in sc:
        copy.start()

    for copy in rc:
        copy.wait_recv()
    group = y * 2 + z // 4
    own_rows = pl.ds(pl.multiple_of(group * 16, 16), 16)
    own_group = section_ref[group] == 0
    spot = lax.broadcasted_iota(jnp.int32, (CACHE, 16), 0) - lax.broadcasted_iota(jnp.int32, (CACHE, 16), 1)
    pick = jnp.where(spot == count_ref[0], 1.0, 0.0).astype(BF16)
    row = lax.broadcasted_iota(jnp.int32, (CACHE, 256), 0) - count_ref[0]
    fresh = (row >= 0) & (row < 16)
    for i, (buf, old, new) in enumerate(((kbuf, ck_ref, nck_ref), (vbuf, cv_ref, ncv_ref))):
        got = jnp.where(own_group, buf[0, 0, own_rows].astype(F32), 0.0)
        for j, dev in enumerate(col_dev):
            got = jnp.where(section_ref[dev[0] // 16] == 0, rbuf[i, j].astype(F32), got)
        moved = jnp.dot(pick, got.astype(BF16), preferred_element_type=F32)
        new[...] = jnp.where(fresh, moved, old[...].astype(F32)).astype(BF16)

    total = sq_s[...]
    for i, copy in enumerate(sc):
        copy.wait_recv()
        total = total + sq_r[i]
    scale = lax.rsqrt(total / (HEADS * HEAD) + 1e-06)
    for h in range(HERE):
        cols = slice(h * HEAD, (h + 1) * HEAD)
        out_ref[:, cols] = o_cur[:, cols] * scale * gain_ref[:, cols]

    for d in (0, 1):
        for step in range(4):
            for p in (0, 1):
                if step < 3 or p == d:
                    q_copy(d, step, p).wait_send()
                if step > 0 or p == d:
                    o_copy(d, step, p).wait_send()
    for copy in list(kc.values()) + list(vc.values()) + rc + sc:
        copy.wait_send()


def on_device(queries, keys, values, cache_keys, cache_values, cache_count, span_section, norm_gain):
    vmem = pl.BlockSpec(memory_space=pltpu.VMEM)
    smem = pl.BlockSpec(memory_space=pltpu.SMEM)
    dma = pltpu.SemaphoreType.DMA
    return pl.pallas_call(
        kernel,
        out_shape=[
            jax.ShapeDtypeStruct((TOK, W), F32),
            jax.ShapeDtypeStruct((CACHE, 256), BF16),
            jax.ShapeDtypeStruct((CACHE, 256), BF16),
        ],
        in_specs=[vmem] * 6 + [smem] * 2,
        out_specs=[vmem] * 3,
        scratch_shapes=[
            pltpu.VMEM((NZ, TOK, W), BF16),
            pltpu.VMEM((2, 4, KROWS, 256), BF16),
            pltpu.VMEM((2, 4, KEYS, 256), BF16),
            pltpu.VMEM((2, 3, 16, 256), BF16),
            pltpu.VMEM((2, 2, 1, 4 * KEYS), F32),
            pltpu.VMEM((NZ, TOK, W), F32),
            pltpu.VMEM((NZ, TOK, W), F32),
            pltpu.VMEM((TOK, W), F32),
            pltpu.VMEM((TOK, W), F32),
            pltpu.VMEM((2, 4, TOK, W + HEAD), BF16),
            pltpu.VMEM((2, 4, TOK, W + HEAD), BF16),
            pltpu.VMEM((TOK, HEAD), F32),
            pltpu.VMEM((3, TOK, HEAD), F32),
            dma((2, 4, 2)), dma((2, 4, 2)),
            dma((9,)), dma((9,)),
            dma((8,)), dma((8,)),
            dma((2, 3)), dma((2, 3)),
            dma((2, 4, 2)), dma((2, 4, 2)),
            dma((3,)), dma((3,)),
        ],
        compiler_params=pltpu.CompilerParams(
            collective_id=0, has_side_effects=True, vmem_limit_bytes=56 * 2**20
        ),
    )(queries, keys, values, cache_keys, cache_values, norm_gain.reshape(1, W), cache_count, span_section)


def solution(mesh):
    placed = (
        P("slot", "head"),
        P("slot", "head"),
        P("slot", "head"),
        P("slot", "head"),
        P("slot", "head"),
        P("slot"),
        P(),
        P("head"),
    )
    return jax.shard_map(
        on_device,
        mesh=mesh,
        in_specs=placed,
        out_specs=(P("slot", "head"), P("slot", "head"), P("slot", "head")),
        check_vma=False,
    )
```

time: 480 us -> 78.7 us (0.16)
  waiting for transfers between devices: 279 us -> 0 us
  matrix products: 76 us -> 0 us
  Pallas kernels: 0 us -> 72.5 us
  starting transfers between devices: 40.3 us -> 0 us
  local copies, waits for them, and re-layouts: 40.3 us -> 4.71 us
  other arithmetic: 30.3 us -> 0 us
  blocking collectives: 10 us -> 0 us
    ppermute x26 -> x0, waiting for transfers between devices: 279 us -> none  [from_partner(): return lax.ppermute(block, axis, route)]
    pallas_call x0 -> x1, Pallas kernels: none -> 72.5 us  [on_device(): pl.pallas_call(kernel, out_shape=[jax.ShapeDtypeStruct((TOK, W), F32), ja...]
    dynamic_update_slice x12 -> x0, matrix products: 52.4 us -> none  [head_step(): numer = lax.dynamic_update_slice_in_dim(numer, mixed, start, 1)]
    ppermute x26 -> x0, starting transfers between devices: 40.3 us -> none  [from_partner(): return lax.ppermute(block, axis, route)]
    while x24 -> x0, local copies, waits for them, and re-layouts: 28 us -> none
    dot_general x12 -> x0, matrix products: 23.7 us -> none  [head_step(): jnp.einsum('qd,kd->qk', query_h, key_h, preferred_element_type=jnp.float32)]
    reduce_sum x14 -> x0, other arithmetic: 13.3 us -> none  [the longest x12 12.2 us: head_step(): jnp.sum(expo, axis=1)[:, None]]
    select_n x26 -> x0, other arithmetic: 11.7 us -> none  [the longest x4 4.16 us: on_device(): jnp.where(high, jnp.concatenate([other, gathered]), jnp.concatenate([gath...]
  transfers between devices with their start and end apart: 26 -> 0, of which waited for: 15 -> 0; matrix products, arithmetic and copies ran while one was open for 2% -> 0% of each run, Pallas kernels for 0% -> 0%
where the time goes in v1:
time: 78.7 us; the launch traced here: 78.5 us
  Pallas kernels  72.5 us (92%)
  local copies, waits for them, and re-layouts  4.71 us (6%)
  between operations  1.3 us (2%)
    pallas_call x1, Pallas kernels, on_device(): pl.pallas_call(kernel, out_shape=[jax.ShapeDtypeStruct((TOK, W), F32), ja...  72.5 us
    unnamed x7, local copies, waits for them, and re-layouts  3.41 us

profile of v1, /device:TPU:1, one launch (start us, length us, event | category | flops | bytes accessed | tf_op | source)
XLA Modules:
  0.0 78.5 jit_solution(15649546616956206796)
XLA Ops:
  1.3 1.3 %reshape.9.gain_ref = f32[1,1536]{1,0:T(1,128)} reshape(f32[1536]{0:T(1024)} %param.15) | data formatting | bytes 12288 | tf_op jit(solution)/shard_map/reshape | solution.py:415
  2.6 72.5 %shard_map.103 = (f32[64,1536]{1,0:T(8,128)}, bf16[256,256]{1,0:T(8,128)(2,1)}, bf16[256,256]{1,0:T(8,128)(2,1)}) custom-call(bf16[64,1536]{1,0:T(8,128)(2,1)} %q_ref.1, bf16[64,256]{1,0:T(8,128)(2,1)} %k_ref.1, bf16[64,256]{1,0:T(8,128)(2,1)} %v_ref.1, bf16[256,256]{1,0:T(8,128)(2,1)} %ck_ref.1, bf16[256,256]{1,0:T(8,128)(2,1)} %cv_ref.1, ...), custom_call_target="tpu_custom_call" | custom-call | tf_op jit(solution)/shard_map/pallas_call | solution.py:382
  75.1 0.0 copy-start.1
  75.1 1.8 %copy.15 = f32[64,1536]{1,0:T(8,128)} copy(f32[64,1536]{1,0:T(8,128)} %get-tuple-element.6) | data formatting | bytes 786432
  76.9 0.0 copy-done.1
  76.9 0.0 copy-start
  76.9 0.7 copy.16
  77.5 0.3 copy-done
  77.8 0.7 copy.17
Async XLA Ops:
  75.1 1.8 %copy-start.1 = (bf16[256,256]{1,0:T(8,128)(2,1)S(1)}, bf16[256,256]{1,0:T(8,128)(2,1)}, u32[]{:S(2)}) copy-start(bf16[256,256]{1,0:T(8,128)(2,1)} %get-tuple-element.7) | copy-start | bytes 393220
  76.9 1.0 %copy-start = (bf16[256,256]{1,0:T(8,128)(2,1)S(1)}, bf16[256,256]{1,0:T(8,128)(2,1)}, u32[]{:S(2)}) copy-start(bf16[256,256]{1,0:T(8,128)(2,1)} %get-tuple-element.8) | copy-start | bytes 393220

commit v2 on v0

v2 whole, which is shorter than its diff:
```python
import functools

import jax
import jax.numpy as jnp
from jax import lax
from jax.experimental import pallas as pl
from jax.experimental.pallas import tpu as pltpu
from jax.sharding import PartitionSpec as P

MESH = pl.DeviceIdType.MESH
F32 = jnp.float32
BF16 = jnp.bfloat16

HEADS = 48
HEAD = 128
TOK = 64
CACHE = 256
KEYS = TOK + CACHE
KVR = 2 * KEYS + 16
SHARE = 6
GW = SHARE * HEAD
MW = GW + HEAD
HALF = TOK // 2
PAIR = 2 * SHARE * TOK
SPAN = 4 * KEYS
TILE = 256
C = HEAD ** -0.5 * 1.4426950408889634
NEG = -1e30
NZ, NX = 8, 4
Z_ORDER = (0, 1, 7, 2, 6, 3, 5, 4)
G1_FIRST = (7, 5, 1, 3)
G1_SECOND = (4, 6, 2, 0)
MSG = {}
for _name, _rows in (
    ("y7", 32), ("y5", 32), ("y6", 32), ("y3", 32), ("x1u", 32), ("x1d", 32), ("xx1u", 16), ("xx1d", 16),
    ("x2u0", 32), ("x2u1", 32), ("x2d0", 32), ("x2d1", 32), ("xx2u", 32), ("xx2d", 32), ("yf", 32),
):
    MSG[_name] = (len(MSG), sum(r for _, _, r in MSG.values()), _rows)
MSG_ROWS = sum(r for _, _, r in MSG.values())


def kernel(
    q_ref, k_ref, v_ref, ck_ref, cv_ref, gain_ref, count_ref, section_ref,
    out_ref, nck_ref, ncv_ref,
    qg, kv, bias, acc, l_st, m_st, s0, s1, mx0, mx1, al0, al1,
    sb0, mb0, sb1, mb1, rt_s, rt_y, rz_s, rz_r, sq_s, sq_r,
    zq_send, zq_recv, zk_send, zk_recv, xk_send, xk_recv, xq_send, xq_recv,
    r_send, r_recv, o_send, o_recv, p_send, p_recv, h_send, h_recv,
):
    slot = lax.axis_index("slot")
    head = lax.axis_index("head")
    y = slot // 32
    z = slot // 4 % 8
    x = slot % 4
    zhi = z // 4

    def at(y_, z_, x_):
        return (y_ * 32 + z_ * 4 + x_, head)

    z_dev = (at(y, (z + 1) % NZ, x), at(y, (z + 7) % NZ, x))
    x_dev = (at(y, z, (x + 1) % NX), at(y, z, (x + 3) % NX))
    y_dev = at(1 - y, z, x)
    far_dev = at(y, (z + 4) % NZ, x)
    pair_core = 1 - head % 2
    head_dev = ((slot, head // 2 * 2 + pair_core), (slot, (head + 2) % 4), (slot, (head + 2) % 4 // 2 * 2 + pair_core))

    barrier = pltpu.get_barrier_semaphore()
    peers = z_dev + x_dev + (y_dev,) + head_dev
    for peer in peers:
        pl.semaphore_signal(barrier, inc=1, device_id=peer, device_id_type=MESH)

    for g in (0, 1):
        cols = slice(g * HEAD, (g + 1) * HEAD)
        qg[g, 0] = q_ref[:, g * GW:(g + 1) * GW]
        kv[2 * g, 0, 0:TOK] = k_ref[:, cols]
        kv[2 * g, 0, TOK:KEYS] = ck_ref[:, cols]
        kv[2 * g, 0, KEYS:KEYS + TOK] = v_ref[:, cols]
        kv[2 * g, 0, KEYS + TOK:2 * KEYS] = cv_ref[:, cols]
        kv[2 * g, 0, 2 * KEYS:KVR] = jnp.full((16, HEAD), count_ref[0].astype(F32), F32).astype(BF16)

    def tokens(ref, group):
        return ref[pl.ds(pl.multiple_of(group * 16, 16), 16)]

    for i, group in enumerate(((1 - y) * 2 + zhi, (1 - y) * 2 + 1 - zhi)):
        rt_s[32 * i:32 * i + 16] = tokens(k_ref, group)
        rt_s[32 * i + 16:32 * i + 32] = tokens(v_ref, group)
    m_st[...] = jnp.full(m_st.shape, NEG, F32)
    l_st[...] = jnp.zeros(l_st.shape, F32)
    acc[...] = jnp.zeros(acc.shape, F32)
    pl.semaphore_wait(barrier, len(peers))

    def remote(src, dst, send, recv, dev):
        return pltpu.make_async_remote_copy(
            src_ref=src, dst_ref=dst, send_sem=send, recv_sem=recv, device_id=dev, device_id_type=MESH
        )

    def zq_view(e, p):
        return qg.at[0, e, p * HALF:(p + 1) * HALF]

    def zk_view(e, p):
        spot = Z_ORDER.index(e)
        rows = slice(0, KEYS) if p == 0 else slice(KEYS, KVR)
        return kv.at[2 + spot // 4, spot % 4, rows]

    def z_copy(kind, d, step, p):
        view, send, recv = ((zq_view, zq_send, zq_recv), (zk_view, zk_send, zk_recv))[kind]
        src = (-step if d == 0 else step) % NZ
        dst = (-step - 1 if d == 0 else step + 1) % NZ
        return remote(view(src, p), view(dst, p), send.at[d, step, p], recv.at[d, step, p], z_dev[d])

    def z_begin(kind, first):
        for d in (0, 1):
            z_copy(kind, d, 0, d if first else 1 - d).start()

    def z_pass(kind, step, first):
        for d in (0, 1):
            p = d if first else 1 - d
            z_copy(kind, d, step, p).wait_recv()
            if step < 2 or (step == 2 and first):
                z_copy(kind, d, step + 1, p).start()

    def xy_copies(view, cut, quarter, end, send, recv):
        table = {
            "own_up": (0, 1, 0, end, x_dev[0]),
            "own_down": (0, 2, 0, end, x_dev[1]),
            "own_y": (0, 3, 0, end, y_dev),
            "fwd_up": (1, 4, 0, cut, x_dev[0]),
            "fwd_down": (2, 4, cut, end, x_dev[1]),
            "y_up": (3, 5, 0, cut, x_dev[0]),
            "y_down": (3, 6, 0, cut, x_dev[1]),
            "yf_up": (5, 7, 0, quarter, x_dev[0]),
            "yf_down": (6, 7, quarter, cut, x_dev[1]),
            "y_1": (1, 5, cut, end, y_dev),
            "y_2": (2, 6, cut, end, y_dev),
            "y_3": (4, 7, cut, end, y_dev),
        }
        return {
            n: remote(view(s, a, b), view(t, a, b), send.at[i], recv.at[i], dev)
            for i, (n, (s, t, a, b, dev)) in enumerate(table.items())
        }

    xk = xy_copies(lambda s, a, b: kv.at[s // 4, s % 4, a:b], KEYS, KEYS // 2, KVR, xk_send, xk_recv)
    xq = xy_copies(lambda s, a, b: qg.at[1, s, a:b], HALF, HALF // 2, TOK, xq_send, xq_recv)

    def xy_begin(c):
        for n in ("own_up", "own_down", "own_y"):
            c[n].start()

    def xy_pass1(c):
        for n in ("own_up", "own_down"):
            c[n].wait_recv()
        c["fwd_up"].start()
        c["fwd_down"].start()
        c["y_1"].start()
        c["y_2"].start()
        c["own_y"].wait_recv()
        c["y_up"].start()
        c["y_down"].start()

    def xy_pass2(c):
        for n in ("fwd_up", "fwd_down"):
            c[n].wait_recv()
        c["y_3"].start()
        for n in ("y_up", "y_down"):
            c[n].wait_recv()
        c["yf_up"].start()
        c["yf_down"].start()

    def xy_pass3(c):
        for n in ("y_1", "y_2", "y_3", "yf_up", "yf_down"):
            c[n].wait_recv()

    rt_copy = remote(rt_s, rt_y, r_send.at[0], r_recv.at[0], y_dev)
    rz_copy = remote(rz_s, rz_r, r_send.at[1], r_recv.at[1], far_dev)

    def far_retire():
        group = y * 2 + 1 - zhi
        rz_s[0:16] = tokens(k_ref, group)
        rz_s[16:32] = tokens(v_ref, group)
        rt_copy.wait_recv()
        rz_s[32:64] = rt_y[32:64]
        rz_copy.start()

    lane = lax.broadcasted_iota(jnp.int32, (1, SPAN), 1)

    def make_bias(ph):
        for sel in (0, 1):
            if ph < 2:
                mine = section_ref[y * 2 + sel]
            else:
                mine = section_ref[(y + sel) % 2 * 2 + zhi]
            total = jnp.zeros((1, SPAN), F32)
            for s in range(4):
                if ph < 2:
                    block = ph * 4 + s
                    key_group = (y if block in (0, 1, 2, 4) else 1 - y) * 2 + zhi
                else:
                    key_group = y * 2 + (z + Z_ORDER[(ph - 2) * 4 + s]) % NZ // 4
                seen = section_ref[key_group] <= mine
                tok = jnp.where(seen, 0.0, NEG).astype(F32)
                live = kv[ph, s, 2 * KEYS:KVR, :].astype(F32)[0:1, 0:1]
                row = lane - s * KEYS
                dead = jnp.where((row - TOK).astype(F32) >= live, NEG, 0.0)
                here = (row >= 0) & (row < KEYS)
                total = jnp.where(here, jnp.where(row < TOK, tok, dead), total)
            bias[ph, sel] = total

    def pick(j, table):
        if isinstance(j, int):
            return table[j]
        return jnp.where(j == 0, table[0], jnp.where(j == 1, table[1], jnp.where(j == 2, table[2], table[3])))

    def unit(u):
        ph, j = u // 4, u % 4
        g = ph // 2
        if isinstance(u, int):
            where = lambda c, a, b: a if c else b
        else:
            where = jnp.where
        far = where(ph == 0, j + 1, 4 - j)
        c1 = where(g == 0, far, pick(j, G1_FIRST))
        c2 = where(g == 0, where(far == 4, 0, NZ - far), pick(j, G1_SECOND))
        sel = lambda c: where(g == 0, (z + c) % NZ // 4, where((c == 3) | (c > 4), 1, 0))
        return ph, g, c1, c2, sel(c1), sel(c2)

    scores, tops, alphas = (s0, s1), (mx0, mx1), (al0, al1)
    ones = jnp.ones((TILE, HEAD), BF16)

    def key_tile(ph, t, base):
        parts, a = [], t * TILE
        while a < (t + 1) * TILE:
            s = a // KEYS
            b = min((t + 1) * TILE, (s + 1) * KEYS)
            parts.append(kv[ph, s, base + a - s * KEYS:base + b - s * KEYS])
            a = b
        return jnp.concatenate(parts, 0) if len(parts) > 1 else parts[0]

    def stacked(ref, g, c1, c2):
        return jnp.concatenate([ref[g, c, :, h * HEAD:(h + 1) * HEAD] for c in (c1, c2) for h in range(SHARE)], 0)

    def unstack(ref, g, c1, c2, value):
        for i, c in enumerate((c1, c2)):
            for h in range(SHARE):
                r = (i * SHARE + h) * TOK
                ref[g, c, :, h * HEAD:(h + 1) * HEAD] = value[r:r + TOK]

    def score_tile(ctx, buf, t, top):
        (ph, g, c1, c2, b1, b2), q = ctx
        s = lax.dot_general(q, key_tile(ph, t, 0), (((1,), (1,)), ((), ())), preferred_element_type=F32)
        cols = slice(t * TILE, (t + 1) * TILE)
        s = jnp.concatenate(
            [s[:PAIR // 2] + bias[ph, b1, :, cols], s[PAIR // 2:] + bias[ph, b2, :, cols]], 0
        )
        scores[buf][:, cols] = s
        t2 = jnp.maximum(s[:, :HEAD], s[:, HEAD:])
        return t2 if top is None else jnp.maximum(top, t2)

    def score_begin(u):
        info = unit(u)
        return info, stacked(qg, info[1], info[2], info[3])

    def score_end(ctx, buf, top):
        _, g, c1, c2, _, _ = ctx[0]
        old = stacked(m_st, g, c1, c2)
        new = jnp.maximum(old, jnp.broadcast_to(jnp.max(top, axis=1, keepdims=True), (PAIR, HEAD)))
        tops[buf][...] = new
        alphas[buf][...] = jnp.exp2((old - new) * C)
        unstack(m_st, g, c1, c2, new)

    def step(u, buf, ahead):
        ph, g, c1, c2, _, _ = unit(u)
        if ahead:
            ctx = score_begin(u + 1)
        top = None
        new_top = tops[buf][...]
        total = None
        for t in range(SPAN // TILE):
            if ahead:
                top = score_tile(ctx, 1 - buf, t, top)
            s = scores[buf][:, t * TILE:(t + 1) * TILE]
            weight = jnp.concatenate(
                [jnp.exp2((s[:, :HEAD] - new_top) * C), jnp.exp2((s[:, HEAD:] - new_top) * C)], 1
            ).astype(BF16)
            v = jnp.concatenate([key_tile(ph, t, KEYS), ones], 1)
            mixed = jnp.dot(weight, v, preferred_element_type=F32)
            total = mixed if total is None else total + mixed
        alpha = alphas[buf][...]
        unstack(acc, g, c1, c2, stacked(acc, g, c1, c2) * alpha + total[:, :HEAD])
        unstack(l_st, g, c1, c2, stacked(l_st, g, c1, c2) * alpha + total[:, HEAD:])
        if ahead:
            score_end(ctx, 1 - buf, top)

    def gather_piece(g, c, r0, n, messages):
        rows = slice(r0, r0 + n)
        lanes = lax.broadcasted_iota(jnp.int32, (n, HEAD), 1)
        sums = jnp.ones((n, HEAD), F32)
        peak = jnp.zeros((n, HEAD), F32)
        for h in range(SHARE):
            cols = slice(h * HEAD, (h + 1) * HEAD)
            sums = jnp.where(lanes % 16 == h, l_st[g, c, rows, cols], sums)
            peak = jnp.where(lanes % 16 == h, m_st[g, c, rows, cols], peak)
        logs = [peak * C + jnp.log2(sums)]
        for ref, a in messages:
            p = ref[a:a + n, GW:MW].astype(F32)
            logs.append(p + pltpu.roll(p, 16, 1) + pltpu.roll(p, 32, 1) + pltpu.roll(p, 48, 1))
        top = functools.reduce(jnp.maximum, logs)
        weights = [jnp.exp2(item - top) for item in logs]
        total = functools.reduce(jnp.add, weights)
        share = 1.0 / total
        factors = [w * share for w in weights]
        factors[0] = factors[0] / sums
        out = []
        for h in range(SHARE):
            cols = slice(h * HEAD, (h + 1) * HEAD)
            spread = [jnp.broadcast_to(f[:, h:h + 1], (n, HEAD)) for f in factors]
            o = acc[g, c, rows, cols] * spread[0]
            for (ref, a), f in zip(messages, spread[1:]):
                o = o + ref[a:a + n, cols].astype(F32) * f
            out.append(o)
        return out, top + jnp.log2(total)

    def write_piece(dst, a, n, out, logs):
        for h in range(SHARE):
            dst[a:a + n, h * HEAD:(h + 1) * HEAD] = out[h].astype(BF16)
        lanes = lax.broadcasted_iota(jnp.int32, (n, HEAD), 1) // 16 % 4
        first = logs.astype(BF16).astype(F32)
        rest = logs - first
        second = rest.astype(BF16).astype(F32)
        third = rest - second
        parts = jnp.where(lanes == 0, first, jnp.where(lanes == 1, second, jnp.where(lanes == 2, third, 0.0)))
        dst[a:a + n, GW:MW] = parts.astype(BF16)

    def o_copy(d, hop, p):
        rows = slice(p * HALF, (p + 1) * HALF)
        return remote(
            sb0.at[d, hop, rows], mb0.at[d, hop, rows], o_send.at[d, hop, p], o_recv.at[d, hop, p], z_dev[d]
        )

    def ring(hop, first):
        for d in (0, 1):
            p = d if first else 1 - d
            messages = []
            if hop > 1 or (hop == 1 and first):
                o_copy(d, hop - 1, p).wait_recv()
                messages = [(mb0.at[d, hop - 1], p * HALF)]
            c = (4 - hop) if d == 0 else (4 + hop)
            write_piece(sb0.at[d, hop], p * HALF, HALF, *gather_piece(0, c, p * HALF, HALF, messages))
            o_copy(d, hop, p).start()

    def p_copy(name):
        i, a, n = MSG[name]
        dev = y_dev if name[0] == "y" else x_dev[0 if "u" in name else 1]
        return remote(sb1.at[a:a + n], mb1.at[a:a + n], p_send.at[i], p_recv.at[i], dev)

    def arrived(name, skip=0):
        return (mb1, MSG[name][1] + skip)

    def tree(name, c, r0, n, *needs):
        _, a, _ = MSG[name]
        write_piece(sb1, a, n, *gather_piece(1, c, r0, n, [arrived(*need) for need in needs]))
        p_copy(name).start()

    def wait_for(*names):
        for name in names:
            p_copy(name).wait_recv()

    def tree_12():
        tree("y7", 7, 32, 32)
        tree("xx1u", 7, 0, 16)
        tree("xx1d", 7, 16, 16)
        tree("x1u", 4, 0, 32)

    def split(name, c, parts):
        _, a, _ = MSG[name]
        for r0, needs in parts:
            write_piece(sb1, a + r0, 16, *gather_piece(1, c, r0, 16, needs))
        p_copy(name).start()

    def tree_13():
        tree("y5", 5, 32, 32)
        tree("y6", 6, 32, 32)
        wait_for("xx1u", "xx1d")
        split("xx2u", 6, ((0, [arrived("xx1u")]), (16, [])))
        split("xx2d", 5, ((0, []), (16, [arrived("xx1d")])))
        wait_for("y7")
        tree("x1d", 4, 32, 32, ("y7",))

    def tree_14():
        tree("x2d0", 1, 0, 32)
        wait_for("x1u")
        tree("x2u0", 2, 0, 32, ("x1u",))
        wait_for("y6")
        tree("x2u1", 2, 32, 32, ("y6",))
        wait_for("y5", "x1d")
        tree("x2d1", 1, 32, 32, ("y5",), ("x1d",))

    def tree_15():
        wait_for("xx2u", "xx2d")
        tree("yf", 3, 0, 32, ("xx2u",), ("xx2d",))
        tree("y3", 3, 32, 32)

    def finish(g, p, messages):
        out, _ = gather_piece(g, 0, p * HALF, HALF, messages)
        squares = jnp.zeros((HALF, HEAD), F32)
        for h in range(SHARE):
            acc[g, 0, p * HALF:(p + 1) * HALF, h * HEAD:(h + 1) * HEAD] = out[h]
            squares = squares + out[h] * out[h]
        rows = slice(p * HALF, (p + 1) * HALF)
        if g == 0:
            sq_s[rows, :] = squares
        else:
            total = jnp.sum(squares + sq_s[rows, :], axis=1, keepdims=True)
            sq_s[rows, :] = jnp.broadcast_to(total, (HALF, HEAD))

    def finish0():
        for p in (0, 1):
            for d in (0, 1):
                o_copy(d, 3, p).wait_recv()
            finish(0, p, [(mb0.at[d, 3], p * HALF) for d in (0, 1)])

    def retire():
        rz_copy.wait_recv()
        group = y * 2 + zhi
        spot = lax.broadcasted_iota(jnp.int32, (CACHE, 16), 0) - lax.broadcasted_iota(jnp.int32, (CACHE, 16), 1)
        chosen = jnp.where(spot == count_ref[0], 1.0, 0.0).astype(BF16)
        row = lax.broadcasted_iota(jnp.int32, (CACHE, 256), 0) - count_ref[0]
        fresh = (row >= 0) & (row < 16)
        for i, (own, old, new) in enumerate(((k_ref, ck_ref, nck_ref), (v_ref, cv_ref, ncv_ref))):
            got = jnp.where(section_ref[group] == 0, tokens(own, group).astype(F32), 0.0)
            for source, ref, a in (
                ((1 - y) * 2 + zhi, rt_y, 0),
                (y * 2 + 1 - zhi, rz_r, 0),
                ((1 - y) * 2 + 1 - zhi, rz_r, 32),
            ):
                got = jnp.where(section_ref[source] == 0, ref[a + 16 * i:a + 16 * i + 16].astype(F32), got)
            moved = jnp.dot(chosen, got.astype(BF16), preferred_element_type=F32)
            new[...] = jnp.where(fresh, moved, old[...].astype(F32)).astype(BF16)

    def z0(*passes):
        def run():
            for args in passes:
                z_pass(*args)
        return run

    before = {
        1: [z0((0, 2, True), (0, 2, False)), lambda: z_begin(1, False), lambda: xy_begin(xq)],
        2: [z0((0, 3, True)), lambda: xy_pass2(xk)],
        3: [lambda: xy_pass3(xk), lambda: make_bias(1), z0((1, 0, True))],
        4: [z0((1, 0, False)), lambda: xy_pass1(xq)],
        5: [z0((1, 1, True)), far_retire],
        6: [z0((1, 1, False)), lambda: xy_pass2(xq)],
        7: [lambda: xy_pass3(xq), lambda: make_bias(2)],
        8: [z0((1, 2, True))],
        9: [z0((1, 2, False))],
        11: [z0((1, 3, True)), lambda: make_bias(3)],
    }
    after = {
        4: [lambda: ring(0, True)],
        5: [lambda: ring(1, False)],
        6: [lambda: ring(1, True)],
        8: [lambda: ring(2, True), lambda: ring(2, False)],
        10: [lambda: ring(3, True), lambda: ring(3, False), retire],
        12: [tree_12],
        13: [tree_13, finish0],
        14: [tree_14],
        15: [tree_15],
    }

    def events(table, u, parity):
        if isinstance(u, int):
            for event in table.get(u, ()):
                event()
            return
        for at_unit, items in table.items():
            if at_unit % 2 == parity and at_unit < 14:
                @pl.when(u == at_unit)
                def _(items=items):
                    for event in items:
                        event()

    z_begin(0, True)
    xy_begin(xk)
    z_begin(0, False)
    rt_copy.start()
    z_pass(0, 0, True)
    z_pass(0, 0, False)
    z_pass(0, 1, True)
    z_begin(1, True)
    xy_pass1(xk)
    make_bias(0)
    ctx = score_begin(0)
    top = None
    for t in range(SPAN // TILE):
        top = score_tile(ctx, 0, t, top)
    score_end(ctx, 0, top)
    z_pass(0, 1, False)

    def two(i, carry):
        for parity in (0, 1):
            u = 2 * i + parity
            events(before, u, parity)
            step(u, parity, True)
            events(after, u, parity)
        return carry

    lax.fori_loop(0, 7, two, 0)
    events(before, 14, 0)
    step(14, 0, True)
    events(after, 14, 0)
    step(15, 1, False)
    events(after, 15, 1)

    wait_for("x2u0", "x2u1", "x2d0", "x2d1", "y3", "yf")
    for p in (0, 1):
        finish(1, p, [arrived(f"x2u{p}"), arrived(f"x2d{p}"), arrived("yf" if p == 0 else "y3")])
    sc = [remote(sq_s, sq_r.at[i], h_send.at[i], h_recv.at[i], head_dev[i]) for i in range(3)]
    for copy in sc:
        copy.start()
    total = sq_s[...]
    for i, copy in enumerate(sc):
        copy.wait_recv()
        total = total + sq_r[i]
    scale = lax.rsqrt(total / (HEADS * HEAD) + 1e-06)
    for g in (0, 1):
        for h in range(SHARE):
            cols = slice(h * HEAD, (h + 1) * HEAD)
            here = slice(g * GW + h * HEAD, g * GW + (h + 1) * HEAD)
            out_ref[:, here] = acc[g, 0, :, cols] * scale * gain_ref[here].reshape(1, HEAD)

    for d in (0, 1):
        for hop in range(4):
            for p in (0, 1):
                if hop < 3 or p == d:
                    z_copy(0, d, hop, p).wait_send()
                    z_copy(1, d, hop, p).wait_send()
                if hop > 0 or p == d:
                    o_copy(d, hop, p).wait_send()
    for copy in list(xk.values()) + list(xq.values()) + [rt_copy, rz_copy] + sc + [p_copy(n) for n in MSG]:
        copy.wait_send()


def on_device(queries, keys, values, cache_keys, cache_values, cache_count, span_section, norm_gain):
    vmem = pl.BlockSpec(memory_space=pltpu.VMEM)
    smem = pl.BlockSpec(memory_space=pltpu.SMEM)
    dma = pltpu.SemaphoreType.DMA
    state = pltpu.VMEM((2, NZ, TOK, GW), F32)
    return pl.pallas_call(
        kernel,
        out_shape=[
            jax.ShapeDtypeStruct((TOK, 2 * GW), F32),
            jax.ShapeDtypeStruct((CACHE, 256), BF16),
            jax.ShapeDtypeStruct((CACHE, 256), BF16),
        ],
        in_specs=[vmem] * 6 + [smem] * 2,
        out_specs=[vmem] * 3,
        scratch_shapes=[
            pltpu.VMEM((2, NZ, TOK, GW), BF16),
            pltpu.VMEM((4, 4, KVR, HEAD), BF16),
            pltpu.VMEM((4, 2, 1, SPAN), F32),
            state, state, state,
            pltpu.VMEM((PAIR, SPAN), F32), pltpu.VMEM((PAIR, SPAN), F32),
            pltpu.VMEM((PAIR, HEAD), F32), pltpu.VMEM((PAIR, HEAD), F32),
            pltpu.VMEM((PAIR, HEAD), F32), pltpu.VMEM((PAIR, HEAD), F32),
            pltpu.VMEM((2, 4, TOK, MW), BF16), pltpu.VMEM((2, 4, TOK, MW), BF16),
            pltpu.VMEM((MSG_ROWS, MW), BF16), pltpu.VMEM((MSG_ROWS, MW), BF16),
            pltpu.VMEM((64, 256), BF16), pltpu.VMEM((64, 256), BF16),
            pltpu.VMEM((64, 256), BF16), pltpu.VMEM((64, 256), BF16),
            pltpu.VMEM((TOK, HEAD), F32),
            pltpu.VMEM((3, TOK, HEAD), F32),
            dma((2, 4, 2)), dma((2, 4, 2)), dma((2, 4, 2)), dma((2, 4, 2)),
            dma((12,)), dma((12,)), dma((12,)), dma((12,)),
            dma((2,)), dma((2,)),
            dma((2, 4, 2)), dma((2, 4, 2)),
            dma((len(MSG),)), dma((len(MSG),)),
            dma((3,)), dma((3,)),
        ],
        compiler_params=pltpu.CompilerParams(
            collective_id=0, has_side_effects=True, vmem_limit_bytes=56 * 2**20
        ),
    )(queries, keys, values, cache_keys, cache_values, norm_gain, cache_count, span_section)


def solution(mesh):
    placed = (
        P("slot", "head"),
        P("slot", "head"),
        P("slot", "head"),
        P("slot", "head"),
        P("slot", "head"),
        P("slot"),
        P(),
        P("head"),
    )
    return jax.shard_map(
        on_device,
        mesh=mesh,
        in_specs=placed,
        out_specs=(P("slot", "head"), P("slot", "head"), P("slot", "head")),
        check_vma=False,
    )
```

time: 480 us -> 77.2 us (0.16)
  waiting for transfers between devices: 279 us -> 0 us
  matrix products: 76 us -> 0 us
  Pallas kernels: 0 us -> 72.3 us
  starting transfers between devices: 40.3 us -> 0 us
  local copies, waits for them, and re-layouts: 40.3 us -> 3.41 us
  other arithmetic: 30.3 us -> 0 us
  blocking collectives: 10 us -> 0 us
    ppermute x26 -> x0, waiting for transfers between devices: 279 us -> none  [from_partner(): return lax.ppermute(block, axis, route)]
    pallas_call x0 -> x1, Pallas kernels: none -> 72.3 us  [on_device(): pl.pallas_call(kernel, out_shape=[jax.ShapeDtypeStruct((TOK, 2 * GW), F32...]
    dynamic_update_slice x12 -> x0, matrix products: 52.4 us -> none  [head_step(): numer = lax.dynamic_update_slice_in_dim(numer, mixed, start, 1)]
    ppermute x26 -> x0, starting transfers between devices: 40.3 us -> none  [from_partner(): return lax.ppermute(block, axis, route)]
    while x24 -> x0, local copies, waits for them, and re-layouts: 28 us -> none
    dot_general x12 -> x0, matrix products: 23.7 us -> none  [head_step(): jnp.einsum('qd,kd->qk', query_h, key_h, preferred_element_type=jnp.float32)]
    reduce_sum x14 -> x0, other arithmetic: 13.3 us -> none  [the longest x12 12.2 us: head_step(): jnp.sum(expo, axis=1)[:, None]]
    select_n x26 -> x0, other arithmetic: 11.7 us -> none  [the longest x4 4.16 us: on_device(): jnp.where(high, jnp.concatenate([other, gathered]), jnp.concatenate([gath...]
  transfers between devices with their start and end apart: 26 -> 0, of which waited for: 15 -> 0; matrix products, arithmetic and copies ran while one was open for 2% -> 0% of each run, Pallas kernels for 0% -> 0%
where the time goes in v2:
time: 77.2 us; the launch traced here: 77 us
  Pallas kernels  72.3 us (94%)
  local copies, waits for them, and re-layouts  3.41 us (4%)
  between operations  1.3 us (2%)
    pallas_call x1, Pallas kernels, on_device(): pl.pallas_call(kernel, out_shape=[jax.ShapeDtypeStruct((TOK, 2 * GW), F32...  72.3 us
    unnamed x7, local copies, waits for them, and re-layouts  3.41 us

profile of v2, /device:TPU:1, one launch (start us, length us, event | category | flops | bytes accessed | tf_op | source)
XLA Modules:
  0.0 77.0 jit_solution(2842483698637934475)
XLA Ops:
  1.3 72.3 %shard_map.103 = (f32[64,1536]{1,0:T(8,128)}, bf16[256,256]{1,0:T(8,128)(2,1)}, bf16[256,256]{1,0:T(8,128)(2,1)}) custom-call(bf16[64,1536]{1,0:T(8,128)(2,1)} %q_ref.1, bf16[64,256]{1,0:T(8,128)(2,1)} %k_ref.1, bf16[64,256]{1,0:T(8,128)(2,1)} %v_ref.1, bf16[256,256]{1,0:T(8,128)(2,1)} %ck_ref.1, bf16[256,256]{1,0:T(8,128)(2,1)} %cv_ref.1, f32[1536]{0:T(1024)} %gain_ref.1, ...), custom_call_target="tpu_custom_call" | custom-call | tf_op jit(solution)/shard_map/pallas_call | solution.py:547
  73.6 0.0 copy-start.1
  73.6 1.8 %copy.15 = f32[64,1536]{1,0:T(8,128)} copy(f32[64,1536]{1,0:T(8,128)} %get-tuple-element.6) | data formatting | bytes 786432
  75.4 0.0 copy-done.1
  75.4 0.0 copy-start
  75.4 0.7 copy.16
  76.1 0.3 copy-done
  76.4 0.7 copy.17
Async XLA Ops:
  73.6 1.8 %copy-start.1 = (bf16[256,256]{1,0:T(8,128)(2,1)S(1)}, bf16[256,256]{1,0:T(8,128)(2,1)}, u32[]{:S(2)}) copy-start(bf16[256,256]{1,0:T(8,128)(2,1)} %get-tuple-element.7) | copy-start | bytes 393220
  75.4 1.0 %copy-start = (bf16[256,256]{1,0:T(8,128)(2,1)S(1)}, bf16[256,256]{1,0:T(8,128)(2,1)}, u32[]{:S(2)}) copy-start(bf16[256,256]{1,0:T(8,128)(2,1)} %get-tuple-element.8) | copy-start | bytes 393220

commit v3 on v2

--- a/solution.py
+++ b/solution.py
@@ -40,10 +40,10 @@
 
 
 def kernel(
-    q_ref, k_ref, v_ref, ck_ref, cv_ref, gain_ref, count_ref, section_ref,
-    out_ref, nck_ref, ncv_ref,
+    q_hbm, k_hbm, v_hbm, ck_hbm, cv_hbm, gain_hbm, count_ref, section_ref,
+    out_ref, nck_hbm, ncv_hbm,
     qg, kv, bias, acc, l_st, m_st, s0, s1, mx0, mx1, al0, al1,
-    sb0, mb0, sb1, mb1, rt_s, rt_y, rz_s, rz_r, sq_s, sq_r,
+    sb0, mb0, sb1, mb1, rt_s, rt_y, rz_s, rz_r, sq_s, sq_r, gain_ref, cache_s, in_sem, out_sem,
     zq_send, zq_recv, zk_send, zk_recv, xk_send, xk_recv, xq_send, xq_recv,
     r_send, r_recv, o_send, o_recv, p_send, p_recv, h_send, h_recv,
 ):
@@ -69,24 +69,33 @@
     for peer in peers:
         pl.semaphore_signal(barrier, inc=1, device_id=peer, device_id_type=MESH)
 
+    loads = []
     for g in (0, 1):
         cols = slice(g * HEAD, (g + 1) * HEAD)
-        qg[g, 0] = q_ref[:, g * GW:(g + 1) * GW]
-        kv[2 * g, 0, 0:TOK] = k_ref[:, cols]
-        kv[2 * g, 0, TOK:KEYS] = ck_ref[:, cols]
-        kv[2 * g, 0, KEYS:KEYS + TOK] = v_ref[:, cols]
-        kv[2 * g, 0, KEYS + TOK:2 * KEYS] = cv_ref[:, cols]
+        loads += [
+            (q_hbm.at[:, g * GW:(g + 1) * GW], qg.at[g, 0]),
+            (k_hbm.at[:, cols], kv.at[2 * g, 0, 0:TOK]),
+            (ck_hbm.at[:, cols], kv.at[2 * g, 0, TOK:KEYS]),
+            (v_hbm.at[:, cols], kv.at[2 * g, 0, KEYS:KEYS + TOK]),
+            (cv_hbm.at[:, cols], kv.at[2 * g, 0, KEYS + TOK:2 * KEYS]),
+        ]
+    loads.append((gain_hbm, gain_ref))
+    loads = [pltpu.make_async_copy(a, b, in_sem.at[i]) for i, (a, b) in enumerate(loads)]
+    for copy in loads:
+        copy.start()
+    for g in (0, 1):
         kv[2 * g, 0, 2 * KEYS:KVR] = jnp.full((16, HEAD), count_ref[0].astype(F32), F32).astype(BF16)
-
-    def tokens(ref, group):
-        return ref[pl.ds(pl.multiple_of(group * 16, 16), 16)]
+    m_st[...] = jnp.full(m_st.shape, NEG, F32)
+    for copy in loads:
+        copy.wait()
+
+    def tokens(kind, group):
+        rows = pl.ds(pl.multiple_of(kind * KEYS + group * 16, 16), 16)
+        return jnp.concatenate([kv[0, 0, rows], kv[2, 0, rows]], 1)
 
     for i, group in enumerate(((1 - y) * 2 + zhi, (1 - y) * 2 + 1 - zhi)):
-        rt_s[32 * i:32 * i + 16] = tokens(k_ref, group)
-        rt_s[32 * i + 16:32 * i + 32] = tokens(v_ref, group)
-    m_st[...] = jnp.full(m_st.shape, NEG, F32)
-    l_st[...] = jnp.zeros(l_st.shape, F32)
-    acc[...] = jnp.zeros(acc.shape, F32)
+        rt_s[32 * i:32 * i + 16] = tokens(0, group)
+        rt_s[32 * i + 16:32 * i + 32] = tokens(1, group)
     pl.semaphore_wait(barrier, len(peers))
 
     def remote(src, dst, send, recv, dev):
@@ -146,37 +155,27 @@
         for n in ("own_up", "own_down", "own_y"):
             c[n].start()
 
-    def xy_pass1(c):
-        for n in ("own_up", "own_down"):
+    def xy_pass(c, needs, then):
+        for n in needs:
             c[n].wait_recv()
-        c["fwd_up"].start()
-        c["fwd_down"].start()
-        c["y_1"].start()
-        c["y_2"].start()
-        c["own_y"].wait_recv()
-        c["y_up"].start()
-        c["y_down"].start()
-
-    def xy_pass2(c):
-        for n in ("fwd_up", "fwd_down"):
-            c[n].wait_recv()
-        c["y_3"].start()
-        for n in ("y_up", "y_down"):
-            c[n].wait_recv()
-        c["yf_up"].start()
-        c["yf_down"].start()
-
-    def xy_pass3(c):
-        for n in ("y_1", "y_2", "y_3", "yf_up", "yf_down"):
-            c[n].wait_recv()
+        for n in then:
+            c[n].start()
+
+    own_x = (("own_up", "own_down"), ("fwd_up", "fwd_down", "y_1", "y_2"))
+    own_y = (("own_y",), ("y_up", "y_down"))
+    two_x = (("fwd_up", "fwd_down"), ("y_3",))
+    two_y = (("y_up", "y_down"), ("yf_up", "yf_down"))
+    last = (("y_1", "y_2", "y_3", "yf_up", "yf_down"), ())
 
     rt_copy = remote(rt_s, rt_y, r_send.at[0], r_recv.at[0], y_dev)
     rz_copy = remote(rz_s, rz_r, r_send.at[1], r_recv.at[1], far_dev)
 
+    cache_out = [pltpu.make_async_copy(cache_s.at[i], (nck_hbm, ncv_hbm)[i], out_sem.at[i]) for i in (0, 1)]
+
     def far_retire():
         group = y * 2 + 1 - zhi
-        rz_s[0:16] = tokens(k_ref, group)
-        rz_s[16:32] = tokens(v_ref, group)
+        rz_s[0:16] = tokens(0, group)
+        rz_s[16:32] = tokens(1, group)
         rt_copy.wait_recv()
         rz_s[32:64] = rt_y[32:64]
         rz_copy.start()
@@ -211,12 +210,13 @@
         return jnp.where(j == 0, table[0], jnp.where(j == 1, table[1], jnp.where(j == 2, table[2], table[3])))
 
     def unit(u):
-        ph, j = u // 4, u % 4
-        g = ph // 2
         if isinstance(u, int):
             where = lambda c, a, b: a if c else b
         else:
             where = jnp.where
+        g = u // 8
+        ph = where(g == 0, u // 4, 2 + u % 2)
+        j = where(g == 0, u % 4, u % 8 // 2)
         far = where(ph == 0, j + 1, 4 - j)
         c1 = where(g == 0, far, pick(j, G1_FIRST))
         c2 = where(g == 0, where(far == 4, 0, NZ - far), pick(j, G1_SECOND))
@@ -364,40 +364,43 @@
         for name in names:
             p_copy(name).wait_recv()
 
-    def tree_12():
-        tree("y7", 7, 32, 32)
-        tree("xx1u", 7, 0, 16)
-        tree("xx1d", 7, 16, 16)
-        tree("x1u", 4, 0, 32)
-
     def split(name, c, parts):
         _, a, _ = MSG[name]
         for r0, needs in parts:
             write_piece(sb1, a + r0, 16, *gather_piece(1, c, r0, 16, needs))
         p_copy(name).start()
 
-    def tree_13():
+    def tree_far():
+        tree("y7", 7, 32, 32)
+        tree("xx1u", 7, 0, 16)
+        tree("xx1d", 7, 16, 16)
+        tree("x1u", 4, 0, 32)
+
+    def tree_y():
         tree("y5", 5, 32, 32)
         tree("y6", 6, 32, 32)
-        wait_for("xx1u", "xx1d")
+
+    def tree_x():
+        wait_for("xx1u", "xx1d", "y7")
+        tree("x1d", 4, 32, 32, ("y7",))
         split("xx2u", 6, ((0, [arrived("xx1u")]), (16, [])))
         split("xx2d", 5, ((0, []), (16, [arrived("xx1d")])))
-        wait_for("y7")
-        tree("x1d", 4, 32, 32, ("y7",))
-
-    def tree_14():
+
+    def tree_near():
         tree("x2d0", 1, 0, 32)
         wait_for("x1u")
         tree("x2u0", 2, 0, 32, ("x1u",))
+
+    def tree_near2():
         wait_for("y6")
         tree("x2u1", 2, 32, 32, ("y6",))
-        wait_for("y5", "x1d")
-        tree("x2d1", 1, 32, 32, ("y5",), ("x1d",))
-
-    def tree_15():
+
+    def tree_last():
         wait_for("xx2u", "xx2d")
         tree("yf", 3, 0, 32, ("xx2u",), ("xx2d",))
         tree("y3", 3, 32, 32)
+        wait_for("y5", "x1d")
+        tree("x2d1", 1, 32, 32, ("y5",), ("x1d",))
 
     def finish(g, p, messages):
         out, _ = gather_piece(g, 0, p * HALF, HALF, messages)
@@ -425,8 +428,8 @@
         chosen = jnp.where(spot == count_ref[0], 1.0, 0.0).astype(BF16)
         row = lax.broadcasted_iota(jnp.int32, (CACHE, 256), 0) - count_ref[0]
         fresh = (row >= 0) & (row < 16)
-        for i, (own, old, new) in enumerate(((k_ref, ck_ref, nck_ref), (v_ref, cv_ref, ncv_ref))):
-            got = jnp.where(section_ref[group] == 0, tokens(own, group).astype(F32), 0.0)
+        for i in (0, 1):
+            got = jnp.where(section_ref[group] == 0, tokens(i, group).astype(F32), 0.0)
             for source, ref, a in (
                 ((1 - y) * 2 + zhi, rt_y, 0),
                 (y * 2 + 1 - zhi, rz_r, 0),
@@ -434,7 +437,11 @@
             ):
                 got = jnp.where(section_ref[source] == 0, ref[a + 16 * i:a + 16 * i + 16].astype(F32), got)
             moved = jnp.dot(chosen, got.astype(BF16), preferred_element_type=F32)
-            new[...] = jnp.where(fresh, moved, old[...].astype(F32)).astype(BF16)
+            rows = slice(i * KEYS + TOK, (i + 1) * KEYS)
+            old = jnp.concatenate([kv[0, 0, rows], kv[2, 0, rows]], 1)
+            cache_s[i] = jnp.where(fresh, moved, old.astype(F32)).astype(BF16)
+        for copy in cache_out:
+            copy.start()
 
     def z0(*passes):
         def run():
@@ -442,28 +449,32 @@
                 z_pass(*args)
         return run
 
+    def xy(c, *passes):
+        def run():
+            for args in passes:
+                xy_pass(c, *args)
+        return run
+
     before = {
-        1: [z0((0, 2, True), (0, 2, False)), lambda: z_begin(1, False), lambda: xy_begin(xq)],
-        2: [z0((0, 3, True)), lambda: xy_pass2(xk)],
-        3: [lambda: xy_pass3(xk), lambda: make_bias(1), z0((1, 0, True))],
-        4: [z0((1, 0, False)), lambda: xy_pass1(xq)],
-        5: [z0((1, 1, True)), far_retire],
-        6: [z0((1, 1, False)), lambda: xy_pass2(xq)],
-        7: [lambda: xy_pass3(xq), lambda: make_bias(2)],
-        8: [z0((1, 2, True))],
-        9: [z0((1, 2, False))],
-        11: [z0((1, 3, True)), lambda: make_bias(3)],
+        1: [z0((1, 1, True), (0, 2, True)), xy(xk, two_x, two_y), xy(xq, two_x, two_y), z0((0, 2, False))],
+        2: [z0((1, 1, False), (0, 3, True))],
+        3: [z0((1, 2, True)), xy(xk, last), lambda: make_bias(1)],
+        4: [far_retire],
+        7: [z0((1, 2, False)), xy(xq, last), lambda: make_bias(2)],
+        8: [z0((1, 3, True)), lambda: make_bias(3)],
     }
     after = {
         4: [lambda: ring(0, True)],
         5: [lambda: ring(1, False)],
-        6: [lambda: ring(1, True)],
-        8: [lambda: ring(2, True), lambda: ring(2, False)],
-        10: [lambda: ring(3, True), lambda: ring(3, False), retire],
-        12: [tree_12],
-        13: [tree_13, finish0],
-        14: [tree_14],
-        15: [tree_15],
+        7: [lambda: ring(1, True)],
+        8: [lambda: ring(2, False)],
+        9: [tree_far],
+        10: [lambda: ring(2, True)],
+        11: [lambda: ring(3, False), tree_y],
+        12: [tree_x],
+        13: [lambda: ring(3, True), tree_near],
+        14: [tree_near2],
+        15: [tree_last, finish0, retire],
     }
 
     def events(table, u, parity):
@@ -480,19 +491,28 @@
 
     z_begin(0, True)
     xy_begin(xk)
+    rt_copy.start()
+    l_st[...] = jnp.zeros(l_st.shape, F32)
     z_begin(0, False)
-    rt_copy.start()
+    acc[...] = jnp.zeros(acc.shape, F32)
+    z_begin(1, True)
     z_pass(0, 0, True)
+    xy_begin(xq)
+    z_begin(1, False)
     z_pass(0, 0, False)
-    z_pass(0, 1, True)
-    z_begin(1, True)
-    xy_pass1(xk)
+    xy_pass(xk, *own_x)
+    xy_pass(xk, *own_y)
+    z_pass(1, 0, True)
     make_bias(0)
     ctx = score_begin(0)
     top = None
     for t in range(SPAN // TILE):
         top = score_tile(ctx, 0, t, top)
     score_end(ctx, 0, top)
+    xy_pass(xq, *own_x)
+    xy_pass(xq, *own_y)
+    z_pass(0, 1, True)
+    z_pass(1, 0, False)
     z_pass(0, 1, False)
 
     def two(i, carry):
@@ -527,6 +547,8 @@
             here = slice(g * GW + h * HEAD, g * GW + (h + 1) * HEAD)
             out_ref[:, here] = acc[g, 0, :, cols] * scale * gain_ref[here].reshape(1, HEAD)
 
+    for copy in cache_out:
+        copy.wait()
     for d in (0, 1):
         for hop in range(4):
             for p in (0, 1):
@@ -542,6 +564,7 @@
 def on_device(queries, keys, values, cache_keys, cache_values, cache_count, span_section, norm_gain):
     vmem = pl.BlockSpec(memory_space=pltpu.VMEM)
     smem = pl.BlockSpec(memory_space=pltpu.SMEM)
+    hbm = pl.BlockSpec(memory_space=pl.ANY)
     dma = pltpu.SemaphoreType.DMA
     state = pltpu.VMEM((2, NZ, TOK, GW), F32)
     return pl.pallas_call(
@@ -551,8 +574,8 @@
             jax.ShapeDtypeStruct((CACHE, 256), BF16),
             jax.ShapeDtypeStruct((CACHE, 256), BF16),
         ],
-        in_specs=[vmem] * 6 + [smem] * 2,
-        out_specs=[vmem] * 3,
+        in_specs=[hbm] * 6 + [smem] * 2,
+        out_specs=[vmem, hbm, hbm],
         scratch_shapes=[
             pltpu.VMEM((2, NZ, TOK, GW), BF16),
             pltpu.VMEM((4, 4, KVR, HEAD), BF16),
@@ -567,6 +590,9 @@
             pltpu.VMEM((64, 256), BF16), pltpu.VMEM((64, 256), BF16),
             pltpu.VMEM((TOK, HEAD), F32),
             pltpu.VMEM((3, TOK, HEAD), F32),
+            pltpu.VMEM((2 * GW,), F32),
+            pltpu.VMEM((2, CACHE, 256), BF16),
+            dma((11,)), dma((2,)),
             dma((2, 4, 2)), dma((2, 4, 2)), dma((2, 4, 2)), dma((2, 4, 2)),
             dma((12,)), dma((12,)), dma((12,)), dma((12,)),
             dma((2,)), dma((2,)),

time: 77.2 us -> 70.2 us (0.909)
  Pallas kernels: 72.3 us -> 65.4 us
    pallas_call x1, Pallas kernels: 72.3 us -> 65.4 us  [on_device(): pl.pallas_call(kernel, out_shape=[jax.ShapeDtypeStruct((TOK, 2 * GW), F32...]
where the time goes in v3:
time: 70.2 us; the launch traced here: 70.1 us
  Pallas kernels  65.4 us (93%)
  local copies, waits for them, and re-layouts  3.41 us (5%)
  between operations  1.3 us (2%)
    pallas_call x1, Pallas kernels, on_device(): pl.pallas_call(kernel, out_shape=[jax.ShapeDtypeStruct((TOK, 2 * GW), F32...  65.4 us
    unnamed x7, local copies, waits for them, and re-layouts  3.41 us

profile of v3, /device:TPU:1, one launch (start us, length us, event | category | flops | bytes accessed | tf_op | source)
XLA Modules:
  0.0 70.1 jit_solution(15918001730974760624)
XLA Ops:
  1.3 65.4 %shard_map.103 = (f32[64,1536]{1,0:T(8,128)}, bf16[256,256]{1,0:T(8,128)(2,1)}, bf16[256,256]{1,0:T(8,128)(2,1)}) custom-call(bf16[64,1536]{1,0:T(8,128)(2,1)} %q_hbm.1, bf16[64,256]{1,0:T(8,128)(2,1)} %k_hbm.1, bf16[64,256]{1,0:T(8,128)(2,1)} %v_hbm.1, bf16[256,256]{1,0:T(8,128)(2,1)} %ck_hbm.1, bf16[256,256]{1,0:T(8,128)(2,1)} %cv_hbm.1, f32[1536]{0:T(1024)} %gain_hbm.1, ...), custom_call_target="tpu_custom_call" | custom-call | tf_op jit(solution)/shard_map/pallas_call | solution.py:570
  66.6 0.0 copy-start.1
  66.7 1.8 %copy.15 = f32[64,1536]{1,0:T(8,128)} copy(f32[64,1536]{1,0:T(8,128)} %get-tuple-element.6) | data formatting | bytes 786432
  68.5 0.0 copy-done.1
  68.5 0.0 copy-start
  68.5 0.7 copy.16
  69.1 0.3 copy-done
  69.4 0.7 copy.17
Async XLA Ops:
  66.6 1.8 %copy-start.1 = (bf16[256,256]{1,0:T(8,128)(2,1)S(1)}, bf16[256,256]{1,0:T(8,128)(2,1)}, u32[]{:S(2)}) copy-start(bf16[256,256]{1,0:T(8,128)(2,1)} %get-tuple-element.7) | copy-start | bytes 393220
  68.5 1.0 %copy-start = (bf16[256,256]{1,0:T(8,128)(2,1)S(1)}, bf16[256,256]{1,0:T(8,128)(2,1)}, u32[]{:S(2)}) copy-start(bf16[256,256]{1,0:T(8,128)(2,1)} %get-tuple-element.8) | copy-start | bytes 393220

commit v4 on v3

--- a/solution.py
+++ b/solution.py
@@ -40,12 +40,11 @@
 
 
 def kernel(
-    q_hbm, k_hbm, v_hbm, ck_hbm, cv_hbm, gain_hbm, count_ref, section_ref,
-    out_ref, nck_hbm, ncv_hbm,
+    q_hbm, k_hbm, v_hbm, ck_hbm, cv_hbm, count_ref, section_ref,
+    o_ref, total_ref, fresh_ref,
     qg, kv, bias, acc, l_st, m_st, s0, s1, mx0, mx1, al0, al1,
-    sb0, mb0, sb1, mb1, rt_s, rt_y, rz_s, rz_r, sq_s, sq_r, gain_ref, cache_s, in_sem, out_sem,
-    zq_send, zq_recv, zk_send, zk_recv, xk_send, xk_recv, xq_send, xq_recv,
-    r_send, r_recv, o_send, o_recv, p_send, p_recv, h_send, h_recv,
+    sb0, mb0, sb1, mb1, rt_s, rt_y, rz_s, rz_r, sq_p, sq_s, sq_r, in_sem,
+    sent, zq_recv, zk_recv, xk_recv, xq_recv, r_recv, o_recv, p_recv, h_recv,
 ):
     slot = lax.axis_index("slot")
     head = lax.axis_index("head")
@@ -79,7 +78,6 @@
             (v_hbm.at[:, cols], kv.at[2 * g, 0, KEYS:KEYS + TOK]),
             (cv_hbm.at[:, cols], kv.at[2 * g, 0, KEYS + TOK:2 * KEYS]),
         ]
-    loads.append((gain_hbm, gain_ref))
     loads = [pltpu.make_async_copy(a, b, in_sem.at[i]) for i, (a, b) in enumerate(loads)]
     for copy in loads:
         copy.start()
@@ -112,10 +110,10 @@
         return kv.at[2 + spot // 4, spot % 4, rows]
 
     def z_copy(kind, d, step, p):
-        view, send, recv = ((zq_view, zq_send, zq_recv), (zk_view, zk_send, zk_recv))[kind]
+        view, send, recv = ((zq_view, sent.at[0], zq_recv), (zk_view, sent.at[1], zk_recv))[kind]
         src = (-step if d == 0 else step) % NZ
         dst = (-step - 1 if d == 0 else step + 1) % NZ
-        return remote(view(src, p), view(dst, p), send.at[d, step, p], recv.at[d, step, p], z_dev[d])
+        return remote(view(src, p), view(dst, p), send, recv.at[d, step, p], z_dev[d])
 
     def z_begin(kind, first):
         for d in (0, 1):
@@ -144,12 +142,12 @@
             "y_3": (4, 7, cut, end, y_dev),
         }
         return {
-            n: remote(view(s, a, b), view(t, a, b), send.at[i], recv.at[i], dev)
+            n: remote(view(s, a, b), view(t, a, b), send, recv.at[i], dev)
             for i, (n, (s, t, a, b, dev)) in enumerate(table.items())
         }
 
-    xk = xy_copies(lambda s, a, b: kv.at[s // 4, s % 4, a:b], KEYS, KEYS // 2, KVR, xk_send, xk_recv)
-    xq = xy_copies(lambda s, a, b: qg.at[1, s, a:b], HALF, HALF // 2, TOK, xq_send, xq_recv)
+    xk = xy_copies(lambda s, a, b: kv.at[s // 4, s % 4, a:b], KEYS, KEYS // 2, KVR, sent.at[2], xk_recv)
+    xq = xy_copies(lambda s, a, b: qg.at[1, s, a:b], HALF, HALF // 2, TOK, sent.at[3], xq_recv)
 
     def xy_begin(c):
         for n in ("own_up", "own_down", "own_y"):
@@ -167,10 +165,8 @@
     two_y = (("y_up", "y_down"), ("yf_up", "yf_down"))
     last = (("y_1", "y_2", "y_3", "yf_up", "yf_down"), ())
 
-    rt_copy = remote(rt_s, rt_y, r_send.at[0], r_recv.at[0], y_dev)
-    rz_copy = remote(rz_s, rz_r, r_send.at[1], r_recv.at[1], far_dev)
-
-    cache_out = [pltpu.make_async_copy(cache_s.at[i], (nck_hbm, ncv_hbm)[i], out_sem.at[i]) for i in (0, 1)]
+    rt_copy = remote(rt_s, rt_y, sent.at[4], r_recv.at[0], y_dev)
+    rz_copy = remote(rz_s, rz_r, sent.at[5], r_recv.at[1], far_dev)
 
     def far_retire():
         group = y * 2 + 1 - zhi
@@ -333,24 +329,28 @@
     def o_copy(d, hop, p):
         rows = slice(p * HALF, (p + 1) * HALF)
         return remote(
-            sb0.at[d, hop, rows], mb0.at[d, hop, rows], o_send.at[d, hop, p], o_recv.at[d, hop, p], z_dev[d]
+            sb0.at[d, hop, rows], mb0.at[d, hop, rows], sent.at[6], o_recv.at[d, hop, p], z_dev[d]
         )
 
     def ring(hop, first):
+        todo = []
         for d in (0, 1):
             p = d if first else 1 - d
             messages = []
             if hop > 1 or (hop == 1 and first):
                 o_copy(d, hop - 1, p).wait_recv()
                 messages = [(mb0.at[d, hop - 1], p * HALF)]
-            c = (4 - hop) if d == 0 else (4 + hop)
-            write_piece(sb0.at[d, hop], p * HALF, HALF, *gather_piece(0, c, p * HALF, HALF, messages))
+            todo.append((d, p, (4 - hop) if d == 0 else (4 + hop), messages))
+        pieces = [gather_piece(0, c, p * HALF, HALF, messages) for d, p, c, messages in todo]
+        for (d, p, _, _), piece in zip(todo, pieces):
+            write_piece(sb0.at[d, hop], p * HALF, HALF, *piece)
+        for d, p, _, _ in todo:
             o_copy(d, hop, p).start()
 
     def p_copy(name):
         i, a, n = MSG[name]
         dev = y_dev if name[0] == "y" else x_dev[0 if "u" in name else 1]
-        return remote(sb1.at[a:a + n], mb1.at[a:a + n], p_send.at[i], p_recv.at[i], dev)
+        return remote(sb1.at[a:a + n], mb1.at[a:a + n], sent.at[7], p_recv.at[i], dev)
 
     def arrived(name, skip=0):
         return (mb1, MSG[name][1] + skip)
@@ -406,14 +406,14 @@
         out, _ = gather_piece(g, 0, p * HALF, HALF, messages)
         squares = jnp.zeros((HALF, HEAD), F32)
         for h in range(SHARE):
-            acc[g, 0, p * HALF:(p + 1) * HALF, h * HEAD:(h + 1) * HEAD] = out[h]
+            o_ref[p * HALF:(p + 1) * HALF, g * GW + h * HEAD:g * GW + (h + 1) * HEAD] = out[h]
             squares = squares + out[h] * out[h]
         rows = slice(p * HALF, (p + 1) * HALF)
         if g == 0:
-            sq_s[rows, :] = squares
+            sq_p[rows, :] = squares
         else:
-            total = jnp.sum(squares + sq_s[rows, :], axis=1, keepdims=True)
-            sq_s[rows, :] = jnp.broadcast_to(total, (HALF, HEAD))
+            total = jnp.sum(squares + sq_p[rows, :], axis=1, keepdims=True)
+            sq_p[rows, :] = jnp.broadcast_to(total, (HALF, HEAD))
 
     def finish0():
         for p in (0, 1):
@@ -424,10 +424,6 @@
     def retire():
         rz_copy.wait_recv()
         group = y * 2 + zhi
-        spot = lax.broadcasted_iota(jnp.int32, (CACHE, 16), 0) - lax.broadcasted_iota(jnp.int32, (CACHE, 16), 1)
-        chosen = jnp.where(spot == count_ref[0], 1.0, 0.0).astype(BF16)
-        row = lax.broadcasted_iota(jnp.int32, (CACHE, 256), 0) - count_ref[0]
-        fresh = (row >= 0) & (row < 16)
         for i in (0, 1):
             got = jnp.where(section_ref[group] == 0, tokens(i, group).astype(F32), 0.0)
             for source, ref, a in (
@@ -436,12 +432,7 @@
                 ((1 - y) * 2 + 1 - zhi, rz_r, 32),
             ):
                 got = jnp.where(section_ref[source] == 0, ref[a + 16 * i:a + 16 * i + 16].astype(F32), got)
-            moved = jnp.dot(chosen, got.astype(BF16), preferred_element_type=F32)
-            rows = slice(i * KEYS + TOK, (i + 1) * KEYS)
-            old = jnp.concatenate([kv[0, 0, rows], kv[2, 0, rows]], 1)
-            cache_s[i] = jnp.where(fresh, moved, old.astype(F32)).astype(BF16)
-        for copy in cache_out:
-            copy.start()
+            fresh_ref[i] = got.astype(BF16)
 
     def z0(*passes):
         def run():
@@ -533,32 +524,44 @@
     wait_for("x2u0", "x2u1", "x2d0", "x2d1", "y3", "yf")
     for p in (0, 1):
         finish(1, p, [arrived(f"x2u{p}"), arrived(f"x2d{p}"), arrived("yf" if p == 0 else "y3")])
-    sc = [remote(sq_s, sq_r.at[i], h_send.at[i], h_recv.at[i], head_dev[i]) for i in range(3)]
+    rows = jnp.concatenate([sq_p[...], jnp.zeros((HEAD - TOK, HEAD), F32)], 0)
+    sq_s[...] = rows.T[0:8]
+    sc = [remote(sq_s, sq_r.at[i], sent.at[8], h_recv.at[i], head_dev[i]) for i in range(3)]
     for copy in sc:
         copy.start()
     total = sq_s[...]
     for i, copy in enumerate(sc):
         copy.wait_recv()
         total = total + sq_r[i]
-    scale = lax.rsqrt(total / (HEADS * HEAD) + 1e-06)
-    for g in (0, 1):
-        for h in range(SHARE):
-            cols = slice(h * HEAD, (h + 1) * HEAD)
-            here = slice(g * GW + h * HEAD, g * GW + (h + 1) * HEAD)
-            out_ref[:, here] = acc[g, 0, :, cols] * scale * gain_ref[here].reshape(1, HEAD)
-
-    for copy in cache_out:
-        copy.wait()
-    for d in (0, 1):
-        for hop in range(4):
-            for p in (0, 1):
-                if hop < 3 or p == d:
-                    z_copy(0, d, hop, p).wait_send()
-                    z_copy(1, d, hop, p).wait_send()
-                if hop > 0 or p == d:
-                    o_copy(d, hop, p).wait_send()
-    for copy in list(xk.values()) + list(xq.values()) + [rt_copy, rz_copy] + sc + [p_copy(n) for n in MSG]:
-        copy.wait_send()
+    total_ref[...] = jnp.concatenate([total] * 16, 0).T[0:TOK]
+
+    for i, refs in enumerate((
+        (qg.at[0, 0:7],),
+        (kv.at[0], kv.at[1, 0:3]),
+        (kv.at[0], kv.at[1, 0:3]),
+        (qg.at[0, 0:7],),
+        (rt_s,),
+        (rz_s,),
+        (sb0.at[0], sb0.at[1, 0:3]),
+        (sb1,),
+        (sq_r,),
+    )):
+        for ref in refs:
+            pltpu.make_async_copy(ref, ref, sent.at[i]).wait()
+
+
+def finish_kernel(count_ref, o_ref, total_ref, gain_ref, ck_ref, cv_ref, fresh_ref, out_ref, nck_ref, ncv_ref):
+    scale = lax.rsqrt(total_ref[...] / (HEADS * HEAD) + 1e-06)
+    for h in range(2 * SHARE):
+        cols = slice(h * HEAD, (h + 1) * HEAD)
+        out_ref[:, cols] = o_ref[:, cols] * scale * gain_ref[cols].reshape(1, HEAD)
+    spot = lax.broadcasted_iota(jnp.int32, (CACHE, 16), 0) - lax.broadcasted_iota(jnp.int32, (CACHE, 16), 1)
+    chosen = jnp.where(spot == count_ref[0], 1.0, 0.0).astype(BF16)
+    row = lax.broadcasted_iota(jnp.int32, (CACHE, 256), 0) - count_ref[0]
+    fresh = (row >= 0) & (row < 16)
+    for i, (old, new) in enumerate(((ck_ref, nck_ref), (cv_ref, ncv_ref))):
+        moved = jnp.dot(chosen, fresh_ref[i], preferred_element_type=F32)
+        new[...] = jnp.where(fresh, moved, old[...].astype(F32)).astype(BF16)
 
 
 def on_device(queries, keys, values, cache_keys, cache_values, cache_count, span_section, norm_gain):
@@ -567,15 +570,15 @@
     hbm = pl.BlockSpec(memory_space=pl.ANY)
     dma = pltpu.SemaphoreType.DMA
     state = pltpu.VMEM((2, NZ, TOK, GW), F32)
-    return pl.pallas_call(
+    o, total, fresh = pl.pallas_call(
         kernel,
         out_shape=[
             jax.ShapeDtypeStruct((TOK, 2 * GW), F32),
-            jax.ShapeDtypeStruct((CACHE, 256), BF16),
-            jax.ShapeDtypeStruct((CACHE, 256), BF16),
+            jax.ShapeDtypeStruct((TOK, HEAD), F32),
+            jax.ShapeDtypeStruct((2, 16, 256), BF16),
         ],
-        in_specs=[hbm] * 6 + [smem] * 2,
-        out_specs=[vmem, hbm, hbm],
+        in_specs=[hbm] * 5 + [smem] * 2,
+        out_specs=[vmem] * 3,
         scratch_shapes=[
             pltpu.VMEM((2, NZ, TOK, GW), BF16),
             pltpu.VMEM((4, 4, KVR, HEAD), BF16),
@@ -589,21 +592,27 @@
             pltpu.VMEM((64, 256), BF16), pltpu.VMEM((64, 256), BF16),
             pltpu.VMEM((64, 256), BF16), pltpu.VMEM((64, 256), BF16),
             pltpu.VMEM((TOK, HEAD), F32),
-            pltpu.VMEM((3, TOK, HEAD), F32),
-            pltpu.VMEM((2 * GW,), F32),
-            pltpu.VMEM((2, CACHE, 256), BF16),
-            dma((11,)), dma((2,)),
-            dma((2, 4, 2)), dma((2, 4, 2)), dma((2, 4, 2)), dma((2, 4, 2)),
-            dma((12,)), dma((12,)), dma((12,)), dma((12,)),
-            dma((2,)), dma((2,)),
-            dma((2, 4, 2)), dma((2, 4, 2)),
-            dma((len(MSG),)), dma((len(MSG),)),
-            dma((3,)), dma((3,)),
+            pltpu.VMEM((8, HEAD), F32),
+            pltpu.VMEM((3, 8, HEAD), F32),
+            dma((10,)),
+            dma((9,)), dma((2, 4, 2)), dma((2, 4, 2)), dma((12,)), dma((12,)), dma((2,)), dma((2, 4, 2)), dma((len(MSG),)),
+            dma((3,)),
         ],
         compiler_params=pltpu.CompilerParams(
             collective_id=0, has_side_effects=True, vmem_limit_bytes=56 * 2**20
         ),
-    )(queries, keys, values, cache_keys, cache_values, norm_gain, cache_count, span_section)
+    )(queries, keys, values, cache_keys, cache_values, cache_count, span_section)
+    return pl.pallas_call(
+        finish_kernel,
+        out_shape=[
+            jax.ShapeDtypeStruct((TOK, 2 * GW), F32),
+            jax.ShapeDtypeStruct((CACHE, 256), BF16),
+            jax.ShapeDtypeStruct((CACHE, 256), BF16),
+        ],
+        in_specs=[smem] + [vmem] * 6,
+        out_specs=[vmem] * 3,
+        compiler_params=pltpu.CompilerParams(vmem_limit_bytes=56 * 2**20),
+    )(cache_count, o, total, norm_gain, cache_keys, cache_values, fresh)
 
 
 def solution(mesh):

time: 70.2 us -> 66.8 us (0.952)
  local copies, waits for them, and re-layouts: 3.41 us -> 0 us
    unnamed x7 -> x0, local copies, waits for them, and re-layouts: 3.41 us -> none
    pallas_call x1, Pallas kernels: 65.4 us -> 63.2 us  [on_device(): pl.pallas_call(kernel, out_shape=[jax.ShapeDtypeStruct((TOK, 2 * GW), F32...]
    pallas_call x0 -> x1, Pallas kernels: none -> 2.15 us  [on_device(): pl.pallas_call(finish_kernel, out_shape=[jax.ShapeDtypeStruct((TOK, 2 * G...]
where the time goes in v4:
time: 66.8 us; the launch traced here: 66.6 us
  Pallas kernels  65.3 us (98%)
  between operations  1.29 us (2%)
    pallas_call x1, Pallas kernels, on_device(): pl.pallas_call(kernel, out_shape=[jax.ShapeDtypeStruct((TOK, 2 * GW), F32...  63.2 us
    pallas_call x1, Pallas kernels, on_device(): pl.pallas_call(finish_kernel, out_shape=[jax.ShapeDtypeStruct((TOK, 2 * G...  2.15 us

profile of v4, /device:TPU:1, one launch (start us, length us, event | category | flops | bytes accessed | tf_op | source)
XLA Modules:
  0.0 66.6 jit_solution(13467557799994606450)
XLA Ops:
  1.3 63.2 %shard_map.103 = (f32[64,1536]{1,0:T(8,128)}, f32[64,128]{1,0:T(8,128)}, bf16[2,16,256]{2,1,0:T(8,128)(2,1)}) custom-call(bf16[64,1536]{1,0:T(8,128)(2,1)} %q_hbm.1, bf16[64,256]{1,0:T(8,128)(2,1)} %k_hbm.1, bf16[64,256]{1,0:T(8,128)(2,1)} %v_hbm.1, bf16[256,256]{1,0:T(8,128)(2,1)} %ck_ref.1, bf16[256,256]{1,0:T(8,128)(2,1)} %cv_ref.1, ...), custom_call_target="tpu_custom_call" | custom-call | tf_op jit(solution)/shard_map/pallas_call | solution.py:573
  64.5 2.1 %shard_map.104 = (f32[64,1536]{1,0:T(8,128)}, bf16[256,256]{1,0:T(8,128)(2,1)}, bf16[256,256]{1,0:T(8,128)(2,1)}) custom-call(s32[1]{0:T(128)S(6)} %copy.11.count_ref, f32[64,1536]{1,0:T(8,128)} %get-tuple-element.6.o_ref, f32[64,128]{1,0:T(8,128)} %get-tuple-element.7.total_ref, f32[1536]{0:T(1024)} %gain_ref.1, bf16[256,256]{1,0:T(8,128)(2,1)} %ck_ref.1, ...), custom_call_target="tpu_custom_call" | custom-call | tf_op jit(solution)/shard_map/pallas_call | solution.py:605

commit v5 on v4

--- a/solution.py
+++ b/solution.py
@@ -28,8 +28,23 @@
 NEG = -1e30
 NZ, NX = 8, 4
 Z_ORDER = (0, 1, 7, 2, 6, 3, 5, 4)
-G1_FIRST = (7, 5, 1, 3)
-G1_SECOND = (4, 6, 2, 0)
+G0_PAIRS = ((1, 7), (2, 6), (3, 5), (4, 0))
+G1_PAIRS = ((7, 4), (5, 6), (1, 2), (3, 0))
+UNITS = (
+    (0, 0, 0), (0, 0, 1), (0, 0, 2), (1, 0, 2),
+    (1, 0, 3), (0, 0, 3), (0, 1, 3), (1, 0, 0),
+    (1, 1, 0), (0, 1, 2), (1, 0, 1), (1, 1, 1),
+    (0, 1, 1), (1, 1, 2), (0, 1, 0), (1, 1, 3),
+)
+PLAN = (
+    "zq0T", "xkown_x", "xkown_y", "rt", "clear_l", "zq0F", "clear_acc", "zk0T", "xqown_x", "xqown_y",
+    "zq1T", "zk0F", "zq1F", "xkfwd", "xky12", "xkyx", "S", "zk1T", "P", "xqfwd",
+    "xqy12", "xqyx", "zq2T", "zq2F", "S", "zk1F", "P", "zk2T", "zq3T", "xky3",
+    "xkyf", "S", "xqyf", "xqy3", "P", "zk2F", "S", "PS", "zk3T", "PS",
+    "PS", "PS", "o0T", "PS", "far", "PS", "y7", "xx1", "PS", "o1T",
+    "o1F", "PS", "PS", "x1", "y56", "xx2", "PS", "o2T", "o2F", "PS",
+    "PS", "x2", "P", "yf", "o3T", "o3F", "y3",
+)
 MSG = {}
 for _name, _rows in (
     ("y7", 32), ("y5", 32), ("y6", 32), ("y3", 32), ("x1u", 32), ("x1d", 32), ("xx1u", 16), ("xx1d", 16),
@@ -83,7 +98,6 @@
         copy.start()
     for g in (0, 1):
         kv[2 * g, 0, 2 * KEYS:KVR] = jnp.full((16, HEAD), count_ref[0].astype(F32), F32).astype(BF16)
-    m_st[...] = jnp.full(m_st.shape, NEG, F32)
     for copy in loads:
         copy.wait()
 
@@ -114,17 +128,6 @@
         src = (-step if d == 0 else step) % NZ
         dst = (-step - 1 if d == 0 else step + 1) % NZ
         return remote(view(src, p), view(dst, p), send, recv.at[d, step, p], z_dev[d])
-
-    def z_begin(kind, first):
-        for d in (0, 1):
-            z_copy(kind, d, 0, d if first else 1 - d).start()
-
-    def z_pass(kind, step, first):
-        for d in (0, 1):
-            p = d if first else 1 - d
-            z_copy(kind, d, step, p).wait_recv()
-            if step < 2 or (step == 2 and first):
-                z_copy(kind, d, step + 1, p).start()
 
     def xy_copies(view, cut, quarter, end, send, recv):
         table = {
@@ -149,21 +152,44 @@
     xk = xy_copies(lambda s, a, b: kv.at[s // 4, s % 4, a:b], KEYS, KEYS // 2, KVR, sent.at[2], xk_recv)
     xq = xy_copies(lambda s, a, b: qg.at[1, s, a:b], HALF, HALF // 2, TOK, sent.at[3], xq_recv)
 
-    def xy_begin(c):
-        for n in ("own_up", "own_down", "own_y"):
-            c[n].start()
-
-    def xy_pass(c, needs, then):
-        for n in needs:
-            c[n].wait_recv()
-        for n in then:
-            c[n].start()
-
-    own_x = (("own_up", "own_down"), ("fwd_up", "fwd_down", "y_1", "y_2"))
-    own_y = (("own_y",), ("y_up", "y_down"))
-    two_x = (("fwd_up", "fwd_down"), ("y_3",))
-    two_y = (("y_up", "y_down"), ("yf_up", "yf_down"))
-    last = (("y_1", "y_2", "y_3", "yf_up", "yf_down"), ())
+    XY = {
+        "own_x": ("own_up", "own_down"), "own_y": ("own_y",), "fwd": ("fwd_up", "fwd_down"), "y12": ("y_1", "y_2"),
+        "yx": ("y_up", "y_down"), "yf": ("yf_up", "yf_down"), "y3": ("y_3",),
+    }
+    XY_NEEDS = {"fwd": "own_x", "y12": "own_x", "yx": "own_y", "yf": "yx", "y3": "fwd"}
+    TREE = {
+        "y7": ("y7",), "xx1": ("xx1u", "xx1d"), "x1": ("x1u", "x1d"), "y56": ("y5", "y6"), "xx2": ("xx2u", "xx2d"),
+        "x2": ("x2u0", "x2u1", "x2d0", "x2d1"), "yf": ("yf",), "y3": ("y3",),
+    }
+
+    def copies(name):
+        kind, rest = name[:2], name[2:]
+        if kind in ("zq", "zk"):
+            return [z_copy(kind == "zk", d, int(rest[0]), d if rest[1] == "T" else 1 - d) for d in (0, 1)]
+        if kind in ("xk", "xq"):
+            return [(xk if kind == "xk" else xq)[n] for n in XY[rest]]
+        if name[0] == "o":
+            return [o_copy(d, int(name[1]), d if name[2] == "T" else 1 - d) for d in (0, 1)]
+        return [p_copy(n) for n in TREE[name]]
+
+    have = set()
+
+    def need(*names):
+        for name in names:
+            if name not in have:
+                have.add(name)
+                for copy in copies(name):
+                    copy.wait_recv()
+
+    def begin(name):
+        kind, rest = name[:2], name[2:]
+        if kind in ("zq", "zk"):
+            if rest[0] != "0":
+                need(kind + str(int(rest[0]) - 1) + rest[1])
+        elif rest in XY_NEEDS:
+            need(kind + XY_NEEDS[rest])
+        for copy in copies(name):
+            copy.start()
 
     rt_copy = remote(rt_s, rt_y, sent.at[4], r_recv.at[0], y_dev)
     rz_copy = remote(rz_s, rz_r, sent.at[5], r_recv.at[1], far_dev)
@@ -200,24 +226,15 @@
                 total = jnp.where(here, jnp.where(row < TOK, tok, dead), total)
             bias[ph, sel] = total
 
-    def pick(j, table):
-        if isinstance(j, int):
-            return table[j]
-        return jnp.where(j == 0, table[0], jnp.where(j == 1, table[1], jnp.where(j == 2, table[2], table[3])))
-
     def unit(u):
-        if isinstance(u, int):
-            where = lambda c, a, b: a if c else b
+        g, half, j = UNITS[u]
+        if g == 0:
+            c1, c2 = G0_PAIRS[j]
+            sel = lambda c: (z + c) % NZ // 4
         else:
-            where = jnp.where
-        g = u // 8
-        ph = where(g == 0, u // 4, 2 + u % 2)
-        j = where(g == 0, u % 4, u % 8 // 2)
-        far = where(ph == 0, j + 1, 4 - j)
-        c1 = where(g == 0, far, pick(j, G1_FIRST))
-        c2 = where(g == 0, where(far == 4, 0, NZ - far), pick(j, G1_SECOND))
-        sel = lambda c: where(g == 0, (z + c) % NZ // 4, where((c == 3) | (c > 4), 1, 0))
-        return ph, g, c1, c2, sel(c1), sel(c2)
+            c1, c2 = G1_PAIRS[j]
+            sel = lambda c: 1 if c in (3, 5, 6, 7) else 0
+        return 2 * g + half, g, c1, c2, sel(c1), sel(c2)
 
     scores, tops, alphas = (s0, s1), (mx0, mx1), (al0, al1)
     ones = jnp.ones((TILE, HEAD), BF16)
@@ -257,11 +274,20 @@
 
     def score_end(ctx, buf, top):
         _, g, c1, c2, _, _ = ctx[0]
-        old = stacked(m_st, g, c1, c2)
-        new = jnp.maximum(old, jnp.broadcast_to(jnp.max(top, axis=1, keepdims=True), (PAIR, HEAD)))
+        new = jnp.broadcast_to(jnp.max(top, axis=1, keepdims=True), (PAIR, HEAD))
+        if ctx[0][0] % 2:
+            old = stacked(m_st, g, c1, c2)
+            new = jnp.maximum(old, new)
+            alphas[buf][...] = jnp.exp2((old - new) * C)
         tops[buf][...] = new
-        alphas[buf][...] = jnp.exp2((old - new) * C)
         unstack(m_st, g, c1, c2, new)
+
+    def score_alone(u):
+        ctx = score_begin(u)
+        top = None
+        for t in range(SPAN // TILE):
+            top = score_tile(ctx, u % 2, t, top)
+        score_end(ctx, u % 2, top)
 
     def step(u, buf, ahead):
         ph, g, c1, c2, _, _ = unit(u)
@@ -280,9 +306,13 @@
             v = jnp.concatenate([key_tile(ph, t, KEYS), ones], 1)
             mixed = jnp.dot(weight, v, preferred_element_type=F32)
             total = mixed if total is None else total + mixed
-        alpha = alphas[buf][...]
-        unstack(acc, g, c1, c2, stacked(acc, g, c1, c2) * alpha + total[:, :HEAD])
-        unstack(l_st, g, c1, c2, stacked(l_st, g, c1, c2) * alpha + total[:, HEAD:])
+        fresh_acc, fresh_sum = total[:, :HEAD], total[:, HEAD:]
+        if ph % 2:
+            alpha = alphas[buf][...]
+            fresh_acc = stacked(acc, g, c1, c2) * alpha + fresh_acc
+            fresh_sum = stacked(l_st, g, c1, c2) * alpha + fresh_sum
+        unstack(acc, g, c1, c2, fresh_acc)
+        unstack(l_st, g, c1, c2, fresh_sum)
         if ahead:
             score_end(ctx, 1 - buf, top)
 
@@ -338,7 +368,7 @@
             p = d if first else 1 - d
             messages = []
             if hop > 1 or (hop == 1 and first):
-                o_copy(d, hop - 1, p).wait_recv()
+                need(f"o{hop - 1}{'T' if first else 'F'}")
                 messages = [(mb0.at[d, hop - 1], p * HALF)]
             todo.append((d, p, (4 - hop) if d == 0 else (4 + hop), messages))
         pieces = [gather_piece(0, c, p * HALF, HALF, messages) for d, p, c, messages in todo]
@@ -360,47 +390,51 @@
         write_piece(sb1, a, n, *gather_piece(1, c, r0, n, [arrived(*need) for need in needs]))
         p_copy(name).start()
 
-    def wait_for(*names):
-        for name in names:
-            p_copy(name).wait_recv()
-
     def split(name, c, parts):
         _, a, _ = MSG[name]
         for r0, needs in parts:
             write_piece(sb1, a + r0, 16, *gather_piece(1, c, r0, 16, needs))
         p_copy(name).start()
 
-    def tree_far():
+    def tree_y7():
         tree("y7", 7, 32, 32)
+
+    def tree_xx1():
         tree("xx1u", 7, 0, 16)
         tree("xx1d", 7, 16, 16)
+
+    def tree_x1():
         tree("x1u", 4, 0, 32)
-
-    def tree_y():
+        need("y7")
+        tree("x1d", 4, 32, 32, ("y7",))
+
+    def tree_y56():
         tree("y5", 5, 32, 32)
         tree("y6", 6, 32, 32)
 
-    def tree_x():
-        wait_for("xx1u", "xx1d", "y7")
-        tree("x1d", 4, 32, 32, ("y7",))
+    def tree_xx2():
+        need("xx1")
         split("xx2u", 6, ((0, [arrived("xx1u")]), (16, [])))
         split("xx2d", 5, ((0, []), (16, [arrived("xx1d")])))
 
-    def tree_near():
+    def tree_x2():
+        need("x1", "y56")
+        tree("x2u0", 2, 0, 32, ("x1u",))
+        tree("x2u1", 2, 32, 32, ("y6",))
         tree("x2d0", 1, 0, 32)
-        wait_for("x1u")
-        tree("x2u0", 2, 0, 32, ("x1u",))
-
-    def tree_near2():
-        wait_for("y6")
-        tree("x2u1", 2, 32, 32, ("y6",))
-
-    def tree_last():
-        wait_for("xx2u", "xx2d")
+        tree("x2d1", 1, 32, 32, ("y5",), ("x1d",))
+
+    def tree_yf():
+        need("xx2")
         tree("yf", 3, 0, 32, ("xx2u",), ("xx2d",))
+
+    def tree_y3():
         tree("y3", 3, 32, 32)
-        wait_for("y5", "x1d")
-        tree("x2d1", 1, 32, 32, ("y5",), ("x1d",))
+
+    trees = {
+        "y7": tree_y7, "xx1": tree_xx1, "x1": tree_x1, "y56": tree_y56, "xx2": tree_xx2, "x2": tree_x2, "yf": tree_yf,
+        "y3": tree_y3,
+    }
 
     def finish(g, p, messages):
         out, _ = gather_piece(g, 0, p * HALF, HALF, messages)
@@ -416,9 +450,8 @@
             sq_p[rows, :] = jnp.broadcast_to(total, (HALF, HEAD))
 
     def finish0():
+        need("o3T", "o3F")
         for p in (0, 1):
-            for d in (0, 1):
-                o_copy(d, 3, p).wait_recv()
             finish(0, p, [(mb0.at[d, 3], p * HALF) for d in (0, 1)])
 
     def retire():
@@ -434,94 +467,56 @@
                 got = jnp.where(section_ref[source] == 0, ref[a + 16 * i:a + 16 * i + 16].astype(F32), got)
             fresh_ref[i] = got.astype(BF16)
 
-    def z0(*passes):
-        def run():
-            for args in passes:
-                z_pass(*args)
-        return run
-
-    def xy(c, *passes):
-        def run():
-            for args in passes:
-                xy_pass(c, *args)
-        return run
-
-    before = {
-        1: [z0((1, 1, True), (0, 2, True)), xy(xk, two_x, two_y), xy(xq, two_x, two_y), z0((0, 2, False))],
-        2: [z0((1, 1, False), (0, 3, True))],
-        3: [z0((1, 2, True)), xy(xk, last), lambda: make_bias(1)],
-        4: [far_retire],
-        7: [z0((1, 2, False)), xy(xq, last), lambda: make_bias(2)],
-        8: [z0((1, 3, True)), lambda: make_bias(3)],
-    }
-    after = {
-        4: [lambda: ring(0, True)],
-        5: [lambda: ring(1, False)],
-        7: [lambda: ring(1, True)],
-        8: [lambda: ring(2, False)],
-        9: [tree_far],
-        10: [lambda: ring(2, True)],
-        11: [lambda: ring(3, False), tree_y],
-        12: [tree_x],
-        13: [lambda: ring(3, True), tree_near],
-        14: [tree_near2],
-        15: [tree_last, finish0, retire],
-    }
-
-    def events(table, u, parity):
-        if isinstance(u, int):
-            for event in table.get(u, ()):
-                event()
-            return
-        for at_unit, items in table.items():
-            if at_unit % 2 == parity and at_unit < 14:
-                @pl.when(u == at_unit)
-                def _(items=items):
-                    for event in items:
-                        event()
-
-    z_begin(0, True)
-    xy_begin(xk)
-    rt_copy.start()
-    l_st[...] = jnp.zeros(l_st.shape, F32)
-    z_begin(0, False)
-    acc[...] = jnp.zeros(acc.shape, F32)
-    z_begin(1, True)
-    z_pass(0, 0, True)
-    xy_begin(xq)
-    z_begin(1, False)
-    z_pass(0, 0, False)
-    xy_pass(xk, *own_x)
-    xy_pass(xk, *own_y)
-    z_pass(1, 0, True)
-    make_bias(0)
-    ctx = score_begin(0)
-    top = None
-    for t in range(SPAN // TILE):
-        top = score_tile(ctx, 0, t, top)
-    score_end(ctx, 0, top)
-    xy_pass(xq, *own_x)
-    xy_pass(xq, *own_y)
-    z_pass(0, 1, True)
-    z_pass(1, 0, False)
-    z_pass(0, 1, False)
-
-    def two(i, carry):
-        for parity in (0, 1):
-            u = 2 * i + parity
-            events(before, u, parity)
-            step(u, parity, True)
-            events(after, u, parity)
-        return carry
-
-    lax.fori_loop(0, 7, two, 0)
-    events(before, 14, 0)
-    step(14, 0, True)
-    events(after, 14, 0)
-    step(15, 1, False)
-    events(after, 15, 1)
-
-    wait_for("x2u0", "x2u1", "x2d0", "x2d1", "y3", "yf")
+    ready = set()
+
+    def unit_needs(u):
+        g, half, j = UNITS[u]
+        if g == 0:
+            need(*[f"zq{k}{p}" for k in range(j + 1) for p in "TF" if k < 3 or p == "T"])
+            need("xkown_x", "xkown_y")
+            if half:
+                need("xkfwd", "xky12", "xkyx", "xkyf", "xky3")
+        else:
+            need("xqown_x", "xqown_y")
+            if j < 2:
+                need("xqfwd", "xqy12", "xqyx", "xqyf", "xqy3")
+            need(*[f"zk{k}{p}" for k in range(4 if half else 2) for p in "TF" if k < 3 or p == "T"])
+        if 2 * g + half not in ready:
+            ready.add(2 * g + half)
+            make_bias(2 * g + half)
+
+    scored = done = 0
+    for op in PLAN:
+        if op == "S":
+            unit_needs(scored)
+            score_alone(scored)
+            scored += 1
+        elif op == "P":
+            step(done, done % 2, False)
+            done += 1
+        elif op == "PS":
+            unit_needs(scored)
+            step(done, done % 2, True)
+            scored += 1
+            done += 1
+        elif op == "clear_l":
+            l_st[...] = jnp.zeros(l_st.shape, F32)
+        elif op == "clear_acc":
+            acc[...] = jnp.zeros(acc.shape, F32)
+        elif op == "rt":
+            rt_copy.start()
+        elif op == "far":
+            need("zq3T")
+            far_retire()
+        elif op in trees:
+            trees[op]()
+        elif op[0] == "o":
+            ring(int(op[1]), op[2] == "T")
+        else:
+            begin(op)
+    finish0()
+    retire()
+    need("x2", "y3", "yf")
     for p in (0, 1):
         finish(1, p, [arrived(f"x2u{p}"), arrived(f"x2d{p}"), arrived("yf" if p == 0 else "y3")])
     rows = jnp.concatenate([sq_p[...], jnp.zeros((HEAD - TOK, HEAD), F32)], 0)

time: 66.8 us -> 63.6 us (0.952)
  Pallas kernels: 65.3 us -> 62.2 us
    pallas_call x1, Pallas kernels: 63.2 us -> 60 us  [on_device(): pl.pallas_call(kernel, out_shape=[jax.ShapeDtypeStruct((TOK, 2 * GW), F32...]
where the time goes in v5:
time: 63.6 us; the launch traced here: 63.5 us
  Pallas kernels  62.2 us (98%)
  between operations  1.29 us (2%)
    pallas_call x1, Pallas kernels, on_device(): pl.pallas_call(kernel, out_shape=[jax.ShapeDtypeStruct((TOK, 2 * GW), F32...  60 us
    pallas_call x1, Pallas kernels, on_device(): pl.pallas_call(finish_kernel, out_shape=[jax.ShapeDtypeStruct((TOK, 2 * G...  2.15 us

profile of v5, /device:TPU:1, one launch (start us, length us, event | category | flops | bytes accessed | tf_op | source)
XLA Modules:
  0.0 63.5 jit_solution(5967656346671072273)
XLA Ops:
  1.3 60.0 %shard_map.103 = (f32[64,1536]{1,0:T(8,128)}, f32[64,128]{1,0:T(8,128)}, bf16[2,16,256]{2,1,0:T(8,128)(2,1)}) custom-call(bf16[64,1536]{1,0:T(8,128)(2,1)} %q_hbm.1, bf16[64,256]{1,0:T(8,128)(2,1)} %k_hbm.1, bf16[64,256]{1,0:T(8,128)(2,1)} %v_hbm.1, bf16[256,256]{1,0:T(8,128)(2,1)} %ck_ref.1, bf16[256,256]{1,0:T(8,128)(2,1)} %cv_ref.1, ...), custom_call_target="tpu_custom_call" | custom-call | tf_op jit(solution)/shard_map/pallas_call | solution.py:568
  61.3 2.1 %shard_map.104 = (f32[64,1536]{1,0:T(8,128)}, bf16[256,256]{1,0:T(8,128)(2,1)}, bf16[256,256]{1,0:T(8,128)(2,1)}) custom-call(s32[1]{0:T(128)S(6)} %copy.11.count_ref, f32[64,1536]{1,0:T(8,128)} %get-tuple-element.6.o_ref, f32[64,128]{1,0:T(8,128)} %get-tuple-element.7.total_ref, f32[1536]{0:T(1024)} %gain_ref.1, bf16[256,256]{1,0:T(8,128)(2,1)} %ck_ref.1, ...), custom_call_target="tpu_custom_call" | custom-call | tf_op jit(solution)/shard_map/pallas_call | solution.py:600

commit v6 on v5

--- a/solution.py
+++ b/solution.py
@@ -55,10 +55,10 @@
 
 
 def kernel(
-    q_hbm, k_hbm, v_hbm, ck_hbm, cv_hbm, count_ref, section_ref,
-    o_ref, total_ref, fresh_ref,
+    q_hbm, k_hbm, v_hbm, ck_hbm, cv_hbm, count_hbm, section_hbm,
+    o_hbm, total_ref, fresh_ref,
     qg, kv, bias, acc, l_st, m_st, s0, s1, mx0, mx1, al0, al1,
-    sb0, mb0, sb1, mb1, rt_s, rt_y, rz_s, rz_r, sq_p, sq_s, sq_r, in_sem,
+    sb0, mb0, sb1, mb1, rt_s, rt_y, rz_s, rz_r, sq_p, sq_s, sq_r, o_ref, count_ref, section_ref, in_sem, out_sem,
     sent, zq_recv, zk_recv, xk_recv, xq_recv, r_recv, o_recv, p_recv, h_recv,
 ):
     slot = lax.axis_index("slot")
@@ -93,12 +93,14 @@
             (v_hbm.at[:, cols], kv.at[2 * g, 0, KEYS:KEYS + TOK]),
             (cv_hbm.at[:, cols], kv.at[2 * g, 0, KEYS + TOK:2 * KEYS]),
         ]
-    loads = [pltpu.make_async_copy(a, b, in_sem.at[i]) for i, (a, b) in enumerate(loads)]
+    scalars = [(count_hbm, count_ref), (section_hbm, section_ref)]
+    loads = [pltpu.make_async_copy(a, b, in_sem.at[i]) for i, (a, b) in enumerate(scalars + loads)]
     for copy in loads:
         copy.start()
+    loads[0].wait()
     for g in (0, 1):
         kv[2 * g, 0, 2 * KEYS:KVR] = jnp.full((16, HEAD), count_ref[0].astype(F32), F32).astype(BF16)
-    for copy in loads:
+    for copy in loads[1:]:
         copy.wait()
 
     def tokens(kind, group):
@@ -448,6 +450,10 @@
         else:
             total = jnp.sum(squares + sq_p[rows, :], axis=1, keepdims=True)
             sq_p[rows, :] = jnp.broadcast_to(total, (HALF, HEAD))
+
+    def o_out(g):
+        cols = slice(g * GW, (g + 1) * GW)
+        return pltpu.make_async_copy(o_ref.at[:, cols], o_hbm.at[:, cols], out_sem.at[g])
 
     def finish0():
         need("o3T", "o3F")
@@ -515,10 +521,12 @@
         else:
             begin(op)
     finish0()
+    o_out(0).start()
     retire()
     need("x2", "y3", "yf")
     for p in (0, 1):
         finish(1, p, [arrived(f"x2u{p}"), arrived(f"x2d{p}"), arrived("yf" if p == 0 else "y3")])
+    o_out(1).start()
     rows = jnp.concatenate([sq_p[...], jnp.zeros((HEAD - TOK, HEAD), F32)], 0)
     sq_s[...] = rows.T[0:8]
     sc = [remote(sq_s, sq_r.at[i], sent.at[8], h_recv.at[i], head_dev[i]) for i in range(3)]
@@ -528,7 +536,9 @@
     for i, copy in enumerate(sc):
         copy.wait_recv()
         total = total + sq_r[i]
-    total_ref[...] = jnp.concatenate([total] * 16, 0).T[0:TOK]
+    total_ref[...] = total
+    for g in (0, 1):
+        o_out(g).wait()
 
     for i, refs in enumerate((
         (qg.at[0, 0:7],),
@@ -546,7 +556,8 @@
 
 
 def finish_kernel(count_ref, o_ref, total_ref, gain_ref, ck_ref, cv_ref, fresh_ref, out_ref, nck_ref, ncv_ref):
-    scale = lax.rsqrt(total_ref[...] / (HEADS * HEAD) + 1e-06)
+    total = jnp.concatenate([total_ref[...]] * 16, 0).T[0:TOK]
+    scale = lax.rsqrt(total / (HEADS * HEAD) + 1e-06)
     for h in range(2 * SHARE):
         cols = slice(h * HEAD, (h + 1) * HEAD)
         out_ref[:, cols] = o_ref[:, cols] * scale * gain_ref[cols].reshape(1, HEAD)
@@ -569,11 +580,11 @@
         kernel,
         out_shape=[
             jax.ShapeDtypeStruct((TOK, 2 * GW), F32),
-            jax.ShapeDtypeStruct((TOK, HEAD), F32),
+            jax.ShapeDtypeStruct((8, HEAD), F32),
             jax.ShapeDtypeStruct((2, 16, 256), BF16),
         ],
-        in_specs=[hbm] * 5 + [smem] * 2,
-        out_specs=[vmem] * 3,
+        in_specs=[hbm] * 7,
+        out_specs=[hbm, vmem, vmem],
         scratch_shapes=[
             pltpu.VMEM((2, NZ, TOK, GW), BF16),
             pltpu.VMEM((4, 4, KVR, HEAD), BF16),
@@ -589,7 +600,10 @@
             pltpu.VMEM((TOK, HEAD), F32),
             pltpu.VMEM((8, HEAD), F32),
             pltpu.VMEM((3, 8, HEAD), F32),
-            dma((10,)),
+            pltpu.VMEM((TOK, 2 * GW), F32),
+            pltpu.SMEM((1,), jnp.int32),
+            pltpu.SMEM((4,), jnp.int32),
+            dma((12,)), dma((2,)),
             dma((9,)), dma((2, 4, 2)), dma((2, 4, 2)), dma((12,)), dma((12,)), dma((2,)), dma((2, 4, 2)), dma((len(MSG),)),
             dma((3,)),
         ],

time: 63.6 us -> 62.7 us (0.986)
  Pallas kernels: 62.2 us -> 61.3 us
    pallas_call x1, Pallas kernels: 60 us -> 59.1 us  [on_device(): pl.pallas_call(kernel, out_shape=[jax.ShapeDtypeStruct((TOK, 2 * GW), F32...]
where the time goes in v6:
time: 62.7 us; the launch traced here: 62.6 us
  Pallas kernels  61.3 us (98%)
  between operations  1.29 us (2%)
    pallas_call x1, Pallas kernels, on_device(): pl.pallas_call(kernel, out_shape=[jax.ShapeDtypeStruct((TOK, 2 * GW), F32...  59.1 us
    pallas_call x1, Pallas kernels, on_device(): pl.pallas_call(finish_kernel, out_shape=[jax.ShapeDtypeStruct((TOK, 2 * G...  2.12 us

profile of v6, /device:TPU:1, one launch (start us, length us, event | category | flops | bytes accessed | tf_op | source)
XLA Modules:
  0.0 62.6 jit_solution(11819792481713186795)
XLA Ops:
  1.3 59.1 %shard_map.103 = (f32[64,1536]{1,0:T(8,128)}, f32[8,128]{1,0:T(8,128)}, bf16[2,16,256]{2,1,0:T(8,128)(2,1)}) custom-call(bf16[64,1536]{1,0:T(8,128)(2,1)} %q_hbm.1, bf16[64,256]{1,0:T(8,128)(2,1)} %k_hbm.1, bf16[64,256]{1,0:T(8,128)(2,1)} %v_hbm.1, bf16[256,256]{1,0:T(8,128)(2,1)} %ck_ref.1, bf16[256,256]{1,0:T(8,128)(2,1)} %cv_ref.1, ...), custom_call_target="tpu_custom_call" | custom-call | tf_op jit(solution)/shard_map/pallas_call | solution.py:579
  60.4 2.1 %shard_map.104 = (f32[64,1536]{1,0:T(8,128)}, bf16[256,256]{1,0:T(8,128)(2,1)}, bf16[256,256]{1,0:T(8,128)(2,1)}) custom-call(s32[1]{0:T(128)S(6)} %copy.11.count_hbm.count_ref, f32[64,1536]{1,0:T(8,128)} %get-tuple-element.6.o_ref, f32[8,128]{1,0:T(8,128)} %get-tuple-element.7.total_ref, f32[1536]{0:T(1024)} %gain_ref.1, bf16[256,256]{1,0:T(8,128)(2,1)} %ck_ref.1, ...), custom_call_target="tpu_custom_call" | custom-call | tf_op jit(solution)/shard_map/pallas_call | solution.py:614

commit v7 on v6

--- a/solution.py
+++ b/solution.py
@@ -31,19 +31,19 @@
 G0_PAIRS = ((1, 7), (2, 6), (3, 5), (4, 0))
 G1_PAIRS = ((7, 4), (5, 6), (1, 2), (3, 0))
 UNITS = (
-    (0, 0, 0), (0, 0, 1), (0, 0, 2), (1, 0, 2),
-    (1, 0, 3), (0, 0, 3), (0, 1, 3), (1, 0, 0),
+    (0, 0, 1), (0, 0, 0), (0, 0, 2), (1, 0, 3),
+    (1, 0, 2), (0, 0, 3), (0, 1, 3), (1, 0, 0),
     (1, 1, 0), (0, 1, 2), (1, 0, 1), (1, 1, 1),
     (0, 1, 1), (1, 1, 2), (0, 1, 0), (1, 1, 3),
 )
 PLAN = (
     "zq0T", "xkown_x", "xkown_y", "rt", "clear_l", "zq0F", "clear_acc", "zk0T", "xqown_x", "xqown_y",
-    "zq1T", "zk0F", "zq1F", "xkfwd", "xky12", "xkyx", "S", "zk1T", "P", "xqfwd",
-    "xqy12", "xqyx", "zq2T", "zq2F", "S", "zk1F", "P", "zk2T", "zq3T", "xky3",
-    "xkyf", "S", "xqyf", "xqy3", "P", "zk2F", "S", "PS", "zk3T", "PS",
-    "PS", "PS", "o0T", "PS", "far", "PS", "y7", "xx1", "PS", "o1T",
-    "o1F", "PS", "PS", "x1", "y56", "xx2", "PS", "o2T", "o2F", "PS",
-    "PS", "x2", "P", "yf", "o3T", "o3F", "y3",
+    "zq1T", "zk0F", "zq1F", "xkfwd", "xky12", "xkyx", "zk1T", "xqfwd", "xqy12", "xqyx",
+    "zq2T", "zq2F", "S", "zk1F", "PS", "zk2T", "P", "xky3", "zq3T", "xkyf",
+    "xqy3", "xqyf", "S", "P", "zk2F", "S", "PS", "zk3T", "PS", "PS",
+    "PS", "o0T", "PS", "far", "PS", "y7", "xx1", "PS", "o1T", "o1F",
+    "PS", "PS", "x1", "y56", "xx2", "PS", "o2T", "o2F", "PS", "PS",
+    "x2", "P", "yf", "y3", "o3T", "o3F",
 )
 MSG = {}
 for _name, _rows in (
@@ -555,19 +555,37 @@
             pltpu.make_async_copy(ref, ref, sent.at[i]).wait()
 
 
-def finish_kernel(count_ref, o_ref, total_ref, gain_ref, ck_ref, cv_ref, fresh_ref, out_ref, nck_ref, ncv_ref):
+def finish_kernel(
+    count_ref, o_hbm, total_ref, gain_ref, ck_hbm, cv_hbm, fresh_ref, out_hbm, nck_hbm, ncv_hbm,
+    o_ref, out_ref, old_ref, new_ref, in_sem, out_sem,
+):
+    blocks = [slice(g * GW, (g + 1) * GW) for g in (0, 1)]
+    loads = [pltpu.make_async_copy(a, old_ref.at[i], in_sem.at[i]) for i, a in enumerate((ck_hbm, cv_hbm))]
+    loads += [pltpu.make_async_copy(o_hbm.at[:, b], o_ref.at[g], in_sem.at[2 + g]) for g, b in enumerate(blocks)]
+    stores = [pltpu.make_async_copy(new_ref.at[i], a, out_sem.at[i]) for i, a in enumerate((nck_hbm, ncv_hbm))]
+    stores += [pltpu.make_async_copy(out_ref.at[g], out_hbm.at[:, b], out_sem.at[2 + g]) for g, b in enumerate(blocks)]
+    for copy in loads:
+        copy.start()
     total = jnp.concatenate([total_ref[...]] * 16, 0).T[0:TOK]
     scale = lax.rsqrt(total / (HEADS * HEAD) + 1e-06)
-    for h in range(2 * SHARE):
-        cols = slice(h * HEAD, (h + 1) * HEAD)
-        out_ref[:, cols] = o_ref[:, cols] * scale * gain_ref[cols].reshape(1, HEAD)
     spot = lax.broadcasted_iota(jnp.int32, (CACHE, 16), 0) - lax.broadcasted_iota(jnp.int32, (CACHE, 16), 1)
     chosen = jnp.where(spot == count_ref[0], 1.0, 0.0).astype(BF16)
     row = lax.broadcasted_iota(jnp.int32, (CACHE, 256), 0) - count_ref[0]
-    fresh = (row >= 0) & (row < 16)
-    for i, (old, new) in enumerate(((ck_ref, nck_ref), (cv_ref, ncv_ref))):
+    inside = (row >= 0) & (row < 16)
+    for i in (0, 1):
+        loads[i].wait()
         moved = jnp.dot(chosen, fresh_ref[i], preferred_element_type=F32)
-        new[...] = jnp.where(fresh, moved, old[...].astype(F32)).astype(BF16)
+        new_ref[i] = jnp.where(inside, moved, old_ref[i].astype(F32)).astype(BF16)
+        stores[i].start()
+    for g in (0, 1):
+        loads[2 + g].wait()
+        for h in range(SHARE):
+            cols = slice(h * HEAD, (h + 1) * HEAD)
+            gain = gain_ref[g * GW + h * HEAD:g * GW + (h + 1) * HEAD].reshape(1, HEAD)
+            out_ref[g, :, cols] = o_ref[g, :, cols] * scale * gain
+        stores[2 + g].start()
+    for copy in stores:
+        copy.wait()
 
 
 def on_device(queries, keys, values, cache_keys, cache_values, cache_count, span_section, norm_gain):
@@ -618,8 +636,13 @@
             jax.ShapeDtypeStruct((CACHE, 256), BF16),
             jax.ShapeDtypeStruct((CACHE, 256), BF16),
         ],
-        in_specs=[smem] + [vmem] * 6,
-        out_specs=[vmem] * 3,
+        in_specs=[smem, hbm, vmem, vmem, hbm, hbm, vmem],
+        out_specs=[hbm] * 3,
+        scratch_shapes=[
+            pltpu.VMEM((2, TOK, GW), F32), pltpu.VMEM((2, TOK, GW), F32),
+            pltpu.VMEM((2, CACHE, 256), BF16), pltpu.VMEM((2, CACHE, 256), BF16),
+            dma((4,)), dma((4,)),
+        ],
         compiler_params=pltpu.CompilerParams(vmem_limit_bytes=56 * 2**20),
     )(cache_count, o, total, norm_gain, cache_keys, cache_values, fresh)
 

time: 62.7 us -> 63.5 us (1.013)
    pallas_call x1, Pallas kernels: 2.12 us -> 2.87 us  [on_device(): pl.pallas_call(finish_kernel, out_shape=[jax.ShapeDtypeStruct((TOK, 2 * G...]
where the time goes in v7:
time: 63.5 us; the launch traced here: 63.3 us
  Pallas kernels  61.8 us (97%)
  between operations  1.47 us (2%)
    pallas_call x1, Pallas kernels, on_device(): pl.pallas_call(kernel, out_shape=[jax.ShapeDtypeStruct((TOK, 2 * GW), F32...  58.9 us
    pallas_call x1, Pallas kernels, on_device(): pl.pallas_call(finish_kernel, out_shape=[jax.ShapeDtypeStruct((TOK, 2 * G...  2.87 us

profile of v7, /device:TPU:1, one launch (start us, length us, event | category | flops | bytes accessed | tf_op | source)
XLA Modules:
  0.0 63.3 jit_solution(15926754706305012166)
XLA Ops:
  1.3 58.9 %shard_map.103 = (f32[64,1536]{1,0:T(8,128)}, f32[8,128]{1,0:T(8,128)}, bf16[2,16,256]{2,1,0:T(8,128)(2,1)}) custom-call(bf16[64,1536]{1,0:T(8,128)(2,1)} %q_hbm.1, bf16[64,256]{1,0:T(8,128)(2,1)} %k_hbm.1, bf16[64,256]{1,0:T(8,128)(2,1)} %v_hbm.1, bf16[256,256]{1,0:T(8,128)(2,1)} %ck_hbm.3, bf16[256,256]{1,0:T(8,128)(2,1)} %cv_hbm.3, ...), custom_call_target="tpu_custom_call" | custom-call | tf_op jit(solution)/shard_map/pallas_call | solution.py:597
  60.2 2.9 %shard_map.104 = (f32[64,1536]{1,0:T(8,128)}, bf16[256,256]{1,0:T(8,128)(2,1)}, bf16[256,256]{1,0:T(8,128)(2,1)}) custom-call(s32[1]{0:T(128)S(6)} %copy.11.count_hbm.count_ref, f32[64,1536]{1,0:T(8,128)} %get-tuple-element.6.o_hbm, f32[8,128]{1,0:T(8,128)} %get-tuple-element.7.total_ref, f32[1536]{0:T(1024)} %gain_ref.1, bf16[256,256]{1,0:T(8,128)(2,1)} %ck_hbm.3, ...), custom_call_target="tpu_custom_call" | custom-call | tf_op jit(solution)/shard_map/pallas_call | solution.py:632
